TPU v7x, 128 devices: a whole 4x4x4 slice. The times are simulated.
128 devices in a mesh: tm: 16 (over y, z), batch: 8 (over x, core).
Axes of the slice: x: 4, y: 4, z: 4, core: 2. Of those that a mesh axis runs over, the one named last changes fastest.
Arguments:
- frames: bfloat16 [8, 8192, 1536], P('batch', 'tm'), may hold values from -12 to 12
- w_query: bfloat16 [1536, 768], replicated, may hold values from -0.15625 to 0.15625
- w_key: bfloat16 [1536, 768], replicated, may hold values from -0.15625 to 0.15625
- w_value: bfloat16 [1536, 768], replicated, may hold values from -0.15625 to 0.15625
- w_out: bfloat16 [768, 1536], replicated, may hold values from -0.21875 to 0.21875
- w_code: bfloat16 [1536, 18], replicated, may hold values from -0.15625 to 0.15625
- code_bias: float32 [18], replicated, may hold values from -1 to 1
- w_expand: bfloat16 [18, 1536], replicated, may hold values from -1.5 to 1.5
- w_up: bfloat16 [2048, 1536], P(('tm', 'batch')), may hold values from -0.15625 to 0.15625
- w_down: bfloat16 [2048, 1536], P(('tm', 'batch')), may hold values from -0.125 to 0.125
- decoder_stream: bfloat16 [8, 8192, 1536], P('batch', 'tm'), may hold values from -6 to 6
- cotangent: bfloat16 [8, 8192, 1536], P('batch', 'tm'), may hold values from -6 to 6
Outputs:
- grad_up: float32 [2048, 1536], P(('tm', 'batch'))
- grad_down: float32 [2048, 1536], P(('tm', 'batch'))
- frame_grad: float32 [8, 8192, 18], P('batch', 'tm')
- penalty: float32 [], replicated
All inputs are finite; a program needn't handle non-finite values.
Results may differ from a plain program's by a relative error of at most 0.015.
Values may be sent and summed in bfloat16 or wider, within the bound.
A program may use at most 192 MiB of HBM per device.

v0:
```python
import math

import jax
import jax.numpy as jnp
from jax import lax
from jax.sharding import PartitionSpec as P

HEADS = 6
HD = 128
BITS = 18
BLOCK = 512


EPSILON = 1e-05
ENT_WEIGHT = 2.0
HIGH = lax.Precision.HIGHEST


def carried_in(value, axis, join, neutral):
    count, mine = (lax.axis_size(axis), lax.axis_index(axis))
    pieces = lax.all_gather(value, axis)
    running = jnp.full_like(value, 0) + jnp.asarray(neutral, value.dtype)

    def hop(position, running):
        longer = join(running, pieces[position])
        return jnp.where(position < mine, longer, running)

    return lax.fori_loop(0, count - 1, hop, running)


def gelu_slope(values):
    coeff = math.sqrt(2.0 / math.pi)
    tangent = jnp.tanh(coeff * (values + 0.044715 * values * values * values))
    return 0.5 * (1.0 + tangent) + 0.5 * values * (1.0 - tangent * tangent) * coeff * (
        1.0 + 3.0 * 0.044715 * values * values
    )


def contract_rows(left, right):
    return lax.dot_general(
        left, right, (((0,), (0,)), ((), ())), preferred_element_type=jnp.float32
    )


def contract_cols(left, right):
    return lax.dot_general(
        left, right, (((1,), (1,)), ((), ())), preferred_element_type=jnp.float32
    )


def body(
    frames,
    w_query,
    w_key,
    w_value,
    w_out,
    w_code,
    code_bias,
    w_expand,
    w_up,
    w_down,
    decoder_stream,
    cotangent,
):
    recs, rows, width = frames.shape
    local_rows = recs * rows
    flat = frames.reshape(local_rows, width)
    scale_q = 1.0 / math.sqrt(HD)
    queries = (jnp.dot(flat, w_query, preferred_element_type=jnp.float32) * scale_q).astype(
        jnp.bfloat16
    )
    keys = jnp.dot(flat, w_key, preferred_element_type=jnp.float32).astype(jnp.bfloat16)
    values = jnp.dot(flat, w_value, preferred_element_type=jnp.float32).astype(jnp.bfloat16)
    queries = queries.reshape(recs, rows, HEADS, HD)
    keys = keys.reshape(recs, rows, HEADS, HD)
    values = values.reshape(recs, rows, HEADS, HD)
    block_states = jnp.einsum("rshk,rshv->rhkv", keys, values, preferred_element_type=jnp.float32)
    history = carried_in(
        block_states, "tm", lambda earlier, later: earlier + later, jnp.zeros_like(block_states)
    )
    causal = jnp.arange(BLOCK)[:, None] >= jnp.arange(BLOCK)[None, :]
    scores = jnp.einsum("rthk,rshk->rhts", queries, keys, preferred_element_type=jnp.float32)
    scores = jnp.where(causal, scores, 0.0).astype(jnp.bfloat16)
    local = jnp.einsum("rhts,rshv->rthv", scores, values, preferred_element_type=jnp.float32)
    carried = jnp.einsum("rthk,rhkv->rthv", queries.astype(jnp.float32), history, precision=HIGH)
    pieces = local + carried
    mixed = pieces.reshape(local_rows, HEADS, HD)
    meansq = jnp.mean(mixed * mixed, axis=-1, keepdims=True)
    normed = (
        (mixed * lax.rsqrt(meansq + EPSILON)).astype(jnp.bfloat16).reshape(local_rows, HEADS * HD)
    )
    hidden = (
        flat.astype(jnp.float32) + jnp.dot(normed, w_out, preferred_element_type=jnp.float32)
    ).astype(jnp.bfloat16)
    zvals = jnp.dot(hidden, w_code, preferred_element_type=jnp.float32) + code_bias
    smooth = jnp.tanh(zvals)
    codes = smooth.astype(jnp.bfloat16)
    stream_flat = decoder_stream.reshape(local_rows, width)
    expanded = (
        stream_flat.astype(jnp.float32)
        + jnp.dot(codes, w_expand, preferred_element_type=jnp.float32)
    ).astype(jnp.bfloat16)
    up_whole, down_whole = (
        lax.all_gather(w_up, ("tm", "batch"), axis=0, tiled=True),
        lax.all_gather(w_down, ("tm", "batch"), axis=0, tiled=True),
    )
    pre = contract_cols(expanded, up_whole)
    act = jax.nn.gelu(pre, approximate=True).astype(jnp.bfloat16)
    cot_flat = cotangent.reshape(local_rows, width)
    dact = contract_cols(cot_flat, down_whole)
    dpre = (dact * gelu_slope(pre)).astype(jnp.bfloat16)
    dexpanded = (
        cot_flat.astype(jnp.float32) + jnp.dot(dpre, up_whole, preferred_element_type=jnp.float32)
    ).astype(jnp.bfloat16)
    dcodes = contract_cols(dexpanded, w_expand)
    logp = jax.nn.log_sigmoid(2.0 * zvals)
    logq = jax.nn.log_sigmoid(-2.0 * zvals)
    prob = jax.nn.sigmoid(2.0 * zvals)
    entropy = -(prob * logp + (1.0 - prob) * logq)
    prob_sums, entropy_sum = lax.psum((jnp.sum(prob, axis=0), jnp.sum(entropy)), ("tm", "batch"))
    total_frames = local_rows * lax.axis_size("tm") * lax.axis_size("batch")
    pbar = prob_sums / total_frames
    batch_ent = -jnp.sum(pbar * jnp.log(pbar) + (1.0 - pbar) * jnp.log(1.0 - pbar))
    penalty = entropy_sum / total_frames - batch_ent
    frame_grad = dcodes * (1.0 - smooth * smooth) + ENT_WEIGHT * 2.0 * prob * (1.0 - prob) * (
        -2.0 * zvals - jnp.log(1.0 - pbar) + jnp.log(pbar)
    )
    summed = lax.psum_scatter(
        jnp.concatenate([contract_rows(dpre, expanded), contract_rows(act, cot_flat)], axis=1),
        ("tm", "batch"),
        scatter_dimension=0,
        tiled=True,
    )
    grad_scale = 1.0 / math.sqrt(total_frames)
    grad_up = summed[:, :width] * grad_scale
    grad_down = summed[:, width:] * grad_scale
    return (grad_up, grad_down, frame_grad.reshape(recs, rows, BITS), penalty)


def solution(mesh):
    in_specs = (
        P("batch", "tm", None),
        P(),
        P(),
        P(),
        P(),
        P(),
        P(),
        P(),
        P(("tm", "batch"), None),
        P(("tm", "batch"), None),
        P("batch", "tm", None),
        P("batch", "tm", None),
    )
    out_specs = (P(("tm", "batch"), None), P(("tm", "batch"), None), P("batch", "tm", None), P())
    return jax.shard_map(body, mesh=mesh, in_specs=in_specs, out_specs=out_specs, check_vma=False)
```

profile of v0, /device:TPU:0, one launch (start us, length us, event | category | flops | bytes accessed | tf_op | source)
XLA Modules:
  0.0 530.2 jit_solution(13145621188883940057)
XLA Ops:
  7.2 1.6 copy-done
  8.8 2.8 fusion.44
  11.9 3.5 fusion.41
  15.7 1.2 fusion.68
  18.5 4.4 multiply_convert_fusion
  22.9 1.4 copy.36
  24.4 3.2 fusion.15
  27.6 53.4 %all-gather.9.cloned.1.call-done = f32[96,128,128]{2,1,0:T(8,128)} async-done(((f32[6,128,128]{2,1,0:T(8,128)}), f32[96,128,128]{2,1,0:T(8,128)}) %all-gather.9.cloned.1.call-update) | async-done | bytes 6291472 | tf_op jit(solution)/shard_map/all_gather | solution.py:21
  81.0 17.3 %while.14 = (s32[]{:T(128)}, f32[1,6,128,128]{3,2,1,0:T(8,128)S(1)}, s32[]{:T(128)}, f32[16,1,6,128,128]{4,3,2,1,0:T(8,128)}, s32[]{:T(128)}, /*index=5*/s32[]{:T(128)}) while((s32[]{:T(128)}, f32[1,6,128,128]{3,2,1,0:T(8,128)S(1)}, s32[]{:T(128)}, f32[16,1,6,128,128]{4,3,2,1,0:T(8,128)}, s32[]{:T(128)}, /*index=5*/s32[]{:T(128)}) %tuple.59), condition=%wide.region_1.2_spmd.clone, body=%wide.region_0.1_spmd.clone.sunk | while | flops 294916 | bytes 1179749 | solution.py:28
  83.3 1.1 add_select_fusion.2
  84.4 1.1 add_select_fusion.2
  90.2 1.1 add_select_fusion.2
  91.3 1.1 add_select_fusion.2
  92.5 1.1 add_select_fusion.2
  93.7 1.1 add_select_fusion.2
  98.3 2.4 fusion.30
  100.9 4.7 fusion.57
  105.6 1.8 fusion.19
  107.4 44.5 %all-gather.7.cloned.1.call-done = bf16[2048,1536]{1,0:T(8,128)(2,1)} async-done(((bf16[16,1536]{1,0:T(8,128)(2,1)}), bf16[2048,1536]{1,0:T(8,128)(2,1)}) %all-gather.7.cloned.1.call-update) | async-done | bytes 6291472 | tf_op jit(solution)/shard_map/all_gather | solution.py:104
  151.9 6.0 %fusion.69 = f32[512,2048]{1,0:T(8,128)S(1)} fusion(bf16[512,1536]{1,0:T(8,128)(2,1)} %fusion.19, bf16[2048,1536]{1,0:T(8,128)(2,1)} %all-gather.7.cloned.1.call-done), kind=kOutput, calls=%fused_computation.86 | convolution fusion | flops 3221225472 | bytes 12058624 | tf_op jit(solution)/shard_map/dot_general | solution.py:46
  157.9 2.0 copy-done.10
  160.0 6.5 %fusion.23 = f32[2048,1536]{0,1:T(8,128)} fusion(f32[512,2048]{1,0:T(8,128)S(1)} %fusion.69, bf16[1,512,1536]{2,1,0:T(8,128)(2,1)S(1)} %copy-done.5), kind=kOutput, calls=%fused_computation.31 | convolution fusion | flops 3230662656 | bytes 18350080 | tf_op jit(solution)/shard_map/dot_general | solution.py:40
  166.5 54.4 %all-gather.5.cloned.1.call-done = bf16[2048,1536]{1,0:T(8,128)(2,1)} async-done(((bf16[16,1536]{1,0:T(8,128)(2,1)}), bf16[2048,1536]{1,0:T(8,128)(2,1)}) %all-gather.5.cloned.1.call-update) | async-done | bytes 6291472 | tf_op jit(solution)/shard_map/all_gather | solution.py:105
  220.9 8.5 %fusion.6 = bf16[512,2048]{1,0:T(8,128)(2,1)S(1)} fusion(f32[512,2048]{1,0:T(8,128)} %copy-done.10, bf16[2048,1536]{1,0:T(8,128)(2,1)} %all-gather.5.cloned.1.call-done, bf16[1,512,1536]{2,1,0:T(8,128)(2,1)} %param.25), kind=kOutput, calls=%fused_computation.12 | convolution fusion | flops 3241148416 | bytes 14155776 | tf_op jit(solution)/shard_map/dot_general | solution.py:46
  229.5 3.7 fusion.70
  233.2 12.4 %pad_maximum_fusion = f32[2048,3072]{0,1:T(8,128)} fusion(f32[2048,1536]{0,1:T(8,128)S(1)} %bitcast.90, f32[2048,1536]{0,1:T(8,128)S(1)} %fusion.70), kind=kLoop, calls=%fused_computation.1 | loop fusion | flops 6291456 | bytes 50331648 | tf_op jit(solution)/shard_map/concatenate | solution.py:129
  245.6 24.7 %copy.52 = f32[2048,3072]{1,0:T(8,128)} copy(f32[2048,3072]{0,1:T(8,128)} %pad_maximum_fusion) | data formatting | bytes 50331648
  271.1 62.9 %all-reduce = (f32[18]{0:T(128)S(1)}, f32[]{:T(128)}) all-reduce(f32[18]{0:T(128)S(1)} %get-tuple-element.124, f32[]{:T(128)S(6)} %neg.35), channel_id=1, replica_groups=mesh['tm'=16,'batch'=8] {'tm','batch'}, use_global_device_ids=true, to_apply=%region_5.6 | all-reduce | flops 19 | bytes 152 | tf_op jit(solution)/shard_map/psum | solution.py:120
  335.9 7.5 %fusion.51 = f32[1,512,18]{1,2,0:T(8,128)S(1)} fusion(bf16[18,1536]{1,0:T(8,128)(2,1)S(1)} %copy-done.4, bf16[512,2048]{1,0:T(8,128)(2,1)} %copy-done.9, bf16[2048,1536]{1,0:T(8,128)(2,1)} %all-gather.7.cloned.1.call-done, bf16[1,512,1536]{2,1,0:T(8,128)(2,1)S(1)} %copy-done.6, f32[512,18]{0,1:T(8,128)S(1)} %get-tuple-element.142, ...), kind=kOutput, calls=%fused_computation.56 | convolution fusion | flops 3252034560 | bytes 10090640 | tf_op jit(solution)/shard_map/dot_general | solution.py:46
  344.0 171.0 %reduce-scatter.4.cloned.1.call-done = f32[16,3072]{1,0:T(8,128)} async-done(((f32[2048,3072]{1,0:T(8,128)}), f32[16,3072]{1,0:T(8,128)}) %reduce-scatter.4.cloned.1.call-update) | async-done | bytes 196624
  517.3 2.0 copy.45
  520.5 2.0 copy.44
  (57 shorter events, 17.3 us)
Async XLA Ops:
  7.2 1.7 copy-start
  7.2 73.8 %all-gather.9.cloned.1.call-start = ((), (), s32[]{:S(2)}) async-start(), calls=%async_computation.3 | async-start | bytes 6684672 | tf_op jit(solution)/shard_map/all_gather | solution.py:21
  16.9 135.0 %all-gather.7.cloned.1.call-start = ((), (), s32[]{:S(2)}) async-start(), calls=%async_computation.2 | async-start | bytes 6340608 | tf_op jit(solution)/shard_map/all_gather | solution.py:104
  17.7 203.2 %all-gather.5.cloned.1.call-start = ((), (), s32[]{:S(2)}) async-start(), calls=%async_computation.1 | async-start | bytes 6340608 | tf_op jit(solution)/shard_map/all_gather | solution.py:105
  18.4 496.7 %reduce-scatter.4.cloned.1.call-start = ((), (), s32[]{:S(2)}) async-start(), calls=%async_computation.4 | async-start | bytes 25362432
  98.3 2.6 copy-start.7
  98.3 2.6 copy-start.8
  100.9 4.7 copy-start.2
  100.9 4.7 copy-start.4
  107.4 52.6 %copy-start.5 = (bf16[1,512,1536]{2,1,0:T(8,128)(2,1)S(1)}, bf16[1,512,1536]{2,1,0:T(8,128)(2,1)}, u32[]{:S(2)}) copy-start(bf16[1,512,1536]{2,1,0:T(8,128)(2,1)} %param.25) | copy-start | bytes 4718596
  157.9 2.0 copy-start.10
  166.5 63.0 %copy-start.3 = (bf16[512,1536]{1,0:T(8,128)(2,1)S(1)}, bf16[512,1536]{1,0:T(8,128)(2,1)}, u32[]{:S(2)}) copy-start(bf16[512,1536]{1,0:T(8,128)(2,1)} %fusion.19) | copy-start | bytes 4718596
  220.9 12.3 %slice-start = ((s8[12582912]{0:T(1024)(128)(4,1)}), s8[4194304]{0:T(1024)(128)(4,1)S(1)}, s32[]{:S(2)}) async-start(s8[12582912]{0:T(1024)(128)(4,1)} %bitcast.89), calls=%async_computation.5 | async-start | bytes 8388608
  220.9 12.3 %slice-start.1 = ((s8[12582912]{0:T(1024)(128)(4,1)}), s8[4194304]{0:T(1024)(128)(4,1)S(1)}, s32[]{:S(2)}) async-start(s8[12582912]{0:T(1024)(128)(4,1)} %bitcast.89), calls=%async_computation.6 | async-start | bytes 8388608
  229.5 3.7 copy-start.9
  229.5 3.8 slice-start.2
  270.3 65.6 %copy-start.6 = (bf16[1,512,1536]{2,1,0:T(8,128)(2,1)S(1)}, bf16[1,512,1536]{2,1,0:T(8,128)(2,1)}, u32[]{:S(2)}) copy-start(bf16[1,512,1536]{2,1,0:T(8,128)(2,1)} %param.25) | copy-start | bytes 4718596
  516.0 6.5 %copy-start.1 = (bf16[1536,768]{1,0:T(8,128)(2,1)S(1)}, bf16[1536,768]{1,0:T(8,128)(2,1)}, u32[]{:S(2)}) copy-start(bf16[1536,768]{1,0:T(8,128)(2,1)} %param.16) | copy-start | bytes 7077892
Sparse Core Ops, SparseCore 0:
  17.0 63.8 all-gather.8
  84.1 67.8 all-gather.6
  155.0 65.8 all-gather.4
  270.5 244.5 reduce-scatter.3
where the time goes:
time: 532 us; the launch traced here: 530 us
  waiting for transfers between devices  325 us (61%)
  blocking collectives  62.9 us (12%)
  matrix products  56.1 us (11%)
  local copies, waits for them, and re-layouts  36.5 us (7%)
  other arithmetic  32.1 us (6%)
  between operations  17.2 us (3%)
    unnamed x5, waiting for transfers between devices  172 us
    psum x1, blocking collectives, body(): lax.psum((jnp.sum(prob, axis=0), jnp.sum(entropy)), ('tm', 'batch'))  62.9 us
    all_gather x1, waiting for transfers between devices, body(): lax.all_gather(w_down, ('tm', 'batch'), axis=0, tiled=True)  54.4 us
    all_gather x1, waiting for transfers between devices, carried_in(): pieces = lax.all_gather(value, axis)  53.4 us
    all_gather x1, waiting for transfers between devices, body(): lax.all_gather(w_up, ('tm', 'batch'), axis=0, tiled=True)  44.5 us
    unnamed x34, local copies, waits for them, and re-layouts  33.6 us
    dot_general x3, matrix products, contract_cols(): lax.dot_general(left, right, (((1,), (1,)), ((), ())), preferred_element_...  22 us
    select_n x15, other arithmetic, hop(): return jnp.where(position < mine, longer, running)  17 us
  transfers between devices with their start and end apart: 4, of which 4 were waited for; matrix products, arithmetic and copies ran while one was open for 11% of the time, Pallas kernels for 0%

commit v1 on v0

v1 whole, which is shorter than its diff:
```python
import math

import jax
import jax.numpy as jnp
from jax import lax
from jax.experimental import pallas as pl
from jax.experimental.pallas import tpu as pltpu
from jax.sharding import PartitionSpec as P

HEADS = 6
HD = 128
BITS = 18
PADBITS = 32
BLOCK = 512
D = 1536
INNER = HEADS * HD
UNITS = 1024
PART = 512
EPSILON = 1e-05
ENT_WEIGHT = 2.0
TOTAL = 65536
MESH = pl.DeviceIdType.MESH
BF = jnp.bfloat16
F32 = jnp.float32

ORDER = (("x", "y", "z"), ("y", "z", "x"), ("z", "x", "y"))
AXES = ("y", "z", "x")
REMOTE = 130


def nn(a, b):
    return jnp.dot(a, b, preferred_element_type=F32)


def nt(a, b):
    return lax.dot_general(a, b, (((1,), (1,)), ((), ())), preferred_element_type=F32)


def tn(a, b):
    return lax.dot_general(a, b, (((0,), (0,)), ((), ())), preferred_element_type=F32)


def fused(
    frames, wq, wk, wv, wo, wct, bias, wexp, wup, wdn, stream, cot,
    gup_out, gdn_out, fg_out, pen_out,
    fr, q_w, k_w, v_w, o_w, st, ct, up, dn, q, k, v, mix,
    own_state, a_recv, b_send, b_recv, before, hid, zt, code, dc, dc_recv,
    act, dpre, pre_t, dact_t, gd, gu, r1, s1, r2, s2, r3, ps,
    lsem, ssem, rsem,
):
    t = lax.axis_index("tm")
    b = lax.axis_index("batch")
    y, z = lax.div(t, 4), lax.rem(t, 4)
    x, c = lax.div(b, 2), lax.rem(b, 2)
    pos = {"y": y, "z": z, "x": x}

    def shifted(axis, step):
        return lax.rem(pos[axis] + step + 4, 4)

    def peer(axis, step):
        n = shifted(axis, step)
        if axis == "x":
            return (t, n * 2 + c)
        if axis == "y":
            return (n * 4 + z, b)
        return (y * 4 + n, b)

    partner = (t, x * 2 + 1 - c)
    count = [0]
    sent = []

    def send(src, dst, device):
        i = count[0]
        count[0] += 1
        copy = pltpu.make_async_remote_copy(
            src_ref=src, dst_ref=dst, send_sem=ssem.at[i], recv_sem=rsem.at[i],
            device_id=device, device_id_type=MESH,
        )
        copy.start()
        sent.append(copy)
        return copy

    loads = [0]

    def load(src, dst):
        copy = pltpu.make_async_copy(src, dst, lsem.at[loads[0]])
        loads[0] += 1
        copy.start()
        return copy

    def cols(p):
        return pl.ds(p * PART, PART)

    def at(buf, p, fixed):
        return buf.at[tuple(fixed.get(a, slice(None)) for a in AXES) + (slice(None), cols(p))]

    l_fr = load(frames, fr)
    l_k = load(wk, k_w)
    l_v = load(wv, v_w)
    l_dn = load(wdn, dn.at[y, z, x])
    l_up = load(wup, up.at[y, z, x])
    barrier = pltpu.get_barrier_semaphore()
    for axis in AXES:
        for step in (1, 2, 3):
            pl.semaphore_signal(barrier, inc=1, device_id=peer(axis, step), device_id_type=MESH)
    pl.semaphore_signal(barrier, inc=1, device_id=partner, device_id_type=MESH)
    pl.semaphore_wait(barrier, 10)

    own = {"y": y, "z": z, "x": x}
    ag1 = []
    for p in range(3):
        for step in (1, 2, 3):
            for src, buf in ((wdn, dn), (wup, up)):
                ag1.append(send(src.at[:, cols(p)], at(buf, p, own), peer(ORDER[p][0], step)))
    l_q = load(wq, q_w)
    l_o = load(wo, o_w)
    l_ct = load(cot, ct.at[pl.ds(0, BLOCK)])
    l_st = load(stream, st.at[pl.ds(0, BLOCK)])
    x_ct = send(cot, ct.at[pl.ds(BLOCK, BLOCK)], partner)
    x_st = send(stream, st.at[pl.ds(BLOCK, BLOCK)], partner)

    def project(weights, out, scale):
        def tile(i, carry):
            rows = pl.ds(pl.multiple_of(i * 256, 256), 256)
            value = nn(fr[rows, :], weights[...])
            if scale is not None:
                value = value * scale
            out[rows, :] = value.astype(BF)
            return carry

        lax.fori_loop(0, BLOCK // 256, tile, 0)

    l_fr.wait()
    l_k.wait()
    project(k_w, k, None)
    l_v.wait()
    project(v_w, v, None)

    def head_cols(h):
        return pl.ds(pl.multiple_of(h * HD, HD), HD)

    def state(h, carry):
        own_state[h] = tn(k[:, head_cols(h)], v[:, head_cols(h)]).astype(BF)
        return carry

    lax.fori_loop(0, HEADS, state, 0)
    stage_a = [send(own_state, a_recv.at[step - 1], peer("y", step)) for step in (1, 2, 3)]

    l_dn.wait()
    l_up.wait()
    for copy in ag1:
        copy.wait_recv()
    ag2 = []
    for p in range(3):
        fixed = {a: pos[a] for a in ORDER[p][1:]}
        for step in (1, 2, 3):
            for buf in (dn, up):
                ag2.append(send(at(buf, p, fixed), at(buf, p, fixed), peer(ORDER[p][1], step)))

    l_q.wait()
    project(q_w, q, 1.0 / math.sqrt(HD))

    for copy in stage_a:
        copy.wait_recv()

    def combine_a(h, carry):
        total = jnp.zeros((HD, HD), F32)
        for step in (1, 2, 3):
            total = total + jnp.where(y >= step, a_recv[step - 1, h].astype(F32), 0.0)
        before[h] = total
        b_send[0, h] = (total + own_state[h].astype(F32)).astype(BF)
        b_send[1, h] = total.astype(BF)
        return carry

    lax.fori_loop(0, HEADS, combine_a, 0)
    stage_b = [
        send(b_send.at[lax.div(z + step, 4)], b_recv.at[step - 1], peer("z", step))
        for step in (1, 2, 3)
    ]

    for copy in ag2:
        copy.wait_recv()
    ag3 = []
    for p in range(3):
        axis = ORDER[p][2]
        mine = {axis: pos[axis]}
        for buf in (dn, up):
            pair = [
                send(at(buf, p, mine), at(buf, p, mine), peer(axis, step)) for step in (1, -1)
            ]
            ag3.append(pair)

    for r in range(2):
        width = (r + 1) * 256
        keep = (
            lax.broadcasted_iota(jnp.int32, (256, width), 0) + r * 256
            >= lax.broadcasted_iota(jnp.int32, (256, width), 1)
        )

        def local(h, carry):
            hc = head_cols(h)
            s = nt(q[pl.ds(r * 256, 256), hc], k[pl.ds(0, width), hc])
            s = jnp.where(keep, s, 0.0).astype(BF)
            mix[pl.ds(r * 256, 256), hc] = nn(s, v[pl.ds(0, width), hc])
            return carry

        lax.fori_loop(0, HEADS, local, 0)

    for copy in stage_b:
        copy.wait_recv()
    l_o.wait()

    def carry_in(h, carry):
        total = before[h]
        for step in range(3):
            total = total + b_recv[step, h].astype(F32)
        history = total.astype(BF)
        hc = head_cols(h)
        m = mix[:, hc] + nn(q[:, hc], history)
        meansq = jnp.mean(m * m, axis=-1, keepdims=True)
        q[:, hc] = (m * lax.rsqrt(meansq + EPSILON)).astype(BF)
        return carry

    lax.fori_loop(0, HEADS, carry_in, 0)

    def out_tile(i, carry):
        rows = pl.ds(pl.multiple_of(i * 256, 256), 256)
        hid[rows, :] = (fr[rows, :].astype(F32) + nn(q[rows, :], o_w[...])).astype(BF)
        return carry

    lax.fori_loop(0, 2, out_tile, 0)
    zvals = nt(wct[...], hid[...]) + bias[...]
    zt[...] = zvals
    code[0] = jnp.tanh(zvals).astype(BF)
    x_code = send(code.at[0], code.at[1], partner)

    ag4 = []
    for p in range(3):
        axis = ORDER[p][2]
        pair_dn, pair_up = ag3[2 * p], ag3[2 * p + 1]
        pair_dn[0].wait_recv()
        left = {axis: shifted(axis, -1)}
        ag4.append(send(at(dn, p, left), at(dn, p, left), peer(axis, 1)))
        pair_up[1].wait_recv()
        right = {axis: shifted(axis, 1)}
        ag4.append(send(at(up, p, right), at(up, p, right), peer(axis, -1)))
        pair_dn[1].wait_recv()
        pair_up[0].wait_recv()

    def sums(slot):
        zv = zt[...]
        two = 2.0 * zv
        logp = jax.nn.log_sigmoid(two)
        logq = jax.nn.log_sigmoid(-two)
        prob = jax.nn.sigmoid(two)
        entropy = -(prob * logp + (1.0 - prob) * logq)
        row = lax.broadcasted_iota(jnp.int32, (PADBITS, 1), 0)
        probs = jnp.sum(prob, axis=1, keepdims=True)
        ents = jnp.sum(entropy, axis=1, keepdims=True)
        ent = jnp.sum(jnp.where(row < BITS, ents, 0.0), axis=0, keepdims=True)
        tile = jnp.where(row < BITS, probs, jnp.where(row == 24, ent, 0.0))
        ps[0, slot] = jnp.broadcast_to(tile, (PADBITS, 128))

    sums(c)
    p_core = send(ps.at[0, c], ps.at[0, c], partner)

    l_ct.wait()
    l_st.wait()
    x_st.wait_recv()

    def expand(slot):
        def tile(i, carry):
            tok = pl.multiple_of(i * 256, 256)
            rows = pl.ds(slot * BLOCK + tok, 256)
            grown = tn(code[slot, :, pl.ds(tok, 256)], wexp[...])
            st[rows, :] = (st[rows, :].astype(F32) + grown).astype(BF)
            return carry

        lax.fori_loop(0, 2, tile, 0)

    expand(0)
    x_code.wait_recv()
    expand(1)
    x_ct.wait_recv()

    def ps_send(stage, axis, value):
        ps[stage, pos[axis]] = value
        return [
            send(ps.at[stage, pos[axis]], ps.at[stage, pos[axis]], peer(axis, step))
            for step in (1, 2, 3)
        ]

    def ps_sum(stage):
        return ps[stage, 0] + ps[stage, 1] + ps[stage, 2] + ps[stage, 3]

    p_core.wait_recv()
    p_x = ps_send(1, "x", ps[0, 0] + ps[0, 1])

    for copy in ag4:
        copy.wait_recv()

    up_all = up.reshape(UNITS, D)
    dn_all = dn.reshape(UNITS, D)
    back = nt(wexp[...], up_all[...]).astype(BF)
    coeff = math.sqrt(2.0 / math.pi)

    def forward(i, carry):
        tok = pl.multiple_of(i * 256, 256)
        rows = pl.ds(tok, 256)
        pre_t[...] = nt(up_all[...], st[rows, :])
        dact_t[...] = nt(dn_all[...], ct[rows, :])

        def slab(j, inner):
            us = pl.ds(pl.multiple_of(j * 64, 64), 64)
            val = pre_t[us, :]
            square = val * val
            half = 0.5 * jnp.tanh(val * (square * (coeff * 0.044715) + coeff)) + 0.5
            gelu = val * half
            slope = half + gelu * (1.0 - half) * (square * (6.0 * 0.044715 * coeff) + 2.0 * coeff)
            act[us, rows] = gelu.astype(BF)
            dpre[us, rows] = (dact_t[us, :] * slope).astype(BF)
            return inner

        lax.fori_loop(0, UNITS // 64, slab, 0)
        dc[:, rows] = nn(back, dpre[:, rows])
        return carry

    lax.fori_loop(0, 4, forward, 0)
    x_dc = send(dc.at[:, pl.ds(BLOCK, BLOCK)], dc_recv, partner)

    gd_all = gd.reshape(UNITS, D)
    gu_all = gu.reshape(UNITS, D)

    def gradient(left, right, out, p):
        def tile(i, carry):
            cs = pl.ds(pl.multiple_of(p * PART + i * 256, 256), 256)
            out[:, cs] = nn(left[...], right[:, cs]).astype(BF)
            return carry

        lax.fori_loop(0, PART // 256, tile, 0)

    grads = (gd, gu)
    way = (1, -1)
    far, near, joined = {}, {}, {}

    def first_sends(m, p):
        axis = ORDER[p][2]
        s = way[m]
        far[m, p] = send(
            at(grads[m], p, {axis: shifted(axis, 2)}), r1.at[m, p, 0], peer(axis, s)
        )
        near[m, p] = send(
            at(grads[m], p, {axis: shifted(axis, -s)}), r1.at[m, p, 1], peer(axis, -s)
        )

    def forward_sum(m, p):
        axis = ORDER[p][2]
        s = way[m]
        far[m, p].wait_recv()
        block = at(grads[m], p, {axis: shifted(axis, s)})

        def add(i, carry):
            block[i] = (block[i].astype(F32) + r1[m, p, 0, i].astype(F32)).astype(BF)
            return carry

        lax.fori_loop(0, 4, add, 0)
        joined[m, p] = send(block, r1.at[m, p, 2], peer(axis, s))

    for p in range(3):
        gradient(act, ct, gd_all, p)
        first_sends(0, p)
    for p in range(3):
        gradient(dpre, st, gu_all, p)
        first_sends(1, p)
        forward_sum(0, p)

    for copy in p_x:
        copy.wait_recv()
    p_y = ps_send(2, "y", ps_sum(1))

    for p in range(3):
        forward_sum(1, p)

    second = {}
    for m in range(2):
        for p in range(3):
            axis = ORDER[p][2]
            near[m, p].wait_recv()
            joined[m, p].wait_recv()
            block = at(grads[m], p, {axis: pos[axis]})

            def total1(i, carry):
                s1[m, p, i] = (
                    block[i].astype(F32)
                    + r1[m, p, 1, i].astype(F32)
                    + r1[m, p, 2, i].astype(F32)
                ).astype(BF)
                return carry

            lax.fori_loop(0, 4, total1, 0)
            axis = ORDER[p][1]
            for step in (1, 2, 3):
                n = shifted(axis, step)
                src = s1.at[m, p, n] if p == 0 else s1.at[m, p, :, n]
                second[m, p, step] = send(src, r2.at[m, p, step - 1], peer(axis, step))

    for copy in p_y:
        copy.wait_recv()
    p_z = ps_send(3, "z", ps_sum(2))

    third = {}
    for m in range(2):
        for p in range(3):
            axis = ORDER[p][1]
            for step in (1, 2, 3):
                second[m, p, step].wait_recv()
            mine = s1.at[m, p, pos[axis]] if p == 0 else s1.at[m, p, :, pos[axis]]
            total = mine[...].astype(F32)
            for step in range(3):
                total = total + r2[m, p, step].astype(F32)
            s2[m, p] = total.astype(BF)
            axis = ORDER[p][0]
            for step in (1, 2, 3):
                third[m, p, step] = send(
                    s2.at[m, p, shifted(axis, step)], r3.at[m, p, step - 1], peer(axis, step)
                )

    for copy in p_z:
        copy.wait_recv()
    x_dc.wait_recv()
    sums_all = ps_sum(3)
    row = lax.broadcasted_iota(jnp.int32, (PADBITS, 128), 0)
    pbar = jnp.where(row < BITS, sums_all / TOTAL, 0.5)
    lp, lq = jnp.log(pbar), jnp.log(1.0 - pbar)
    spread = jnp.where(row < BITS, -(pbar * lp + (1.0 - pbar) * lq), 0.0)
    batch_ent = jnp.sum(spread, axis=0, keepdims=True)
    pen_out[...] = jnp.broadcast_to(sums_all[24:25, :] / TOTAL - batch_ent, (8, 128))
    zv = zt[...]
    smooth = jnp.tanh(zv)
    prob = jax.nn.sigmoid(2.0 * zv)
    dcodes = nt(wexp[...], ct[pl.ds(0, BLOCK), :]) + dc[:, pl.ds(0, BLOCK)] + dc_recv[...]
    fg_out[...] = dcodes * (1.0 - smooth * smooth) + ENT_WEIGHT * 2.0 * prob * (1.0 - prob) * (
        -2.0 * zv - lq[:, :1] + lp[:, :1]
    )

    scale = 1.0 / math.sqrt(TOTAL)
    for m, out in ((0, gdn_out), (1, gup_out)):
        for p in range(3):
            axis = ORDER[p][0]
            total = s2[m, p, pos[axis]].astype(F32)
            for step in (1, 2, 3):
                third[m, p, step].wait_recv()
                total = total + r3[m, p, step - 1].astype(F32)
            out[:, cols(p)] = total * scale
    for copy in sent:
        copy.wait_send()


def body(
    frames, w_query, w_key, w_value, w_out, w_code, code_bias, w_expand, w_up, w_down,
    decoder_stream, cotangent,
):
    spare = PADBITS - BITS
    wct = jnp.pad(w_code.T, ((0, spare), (0, 0)))
    wexp = jnp.pad(w_expand, ((0, spare), (0, 0)))
    bias = jnp.pad(code_bias, (0, spare)).reshape(PADBITS, 1)
    anywhere = pl.BlockSpec(memory_space=pl.ANY)
    vmem = pl.BlockSpec(memory_space=pltpu.VMEM)
    state = (HEADS, HD, HD)
    scratch = [
        pltpu.VMEM((BLOCK, D), BF),
        pltpu.VMEM((D, INNER), BF),
        pltpu.VMEM((D, INNER), BF),
        pltpu.VMEM((D, INNER), BF),
        pltpu.VMEM((INNER, D), BF),
        pltpu.VMEM((2 * BLOCK, D), BF),
        pltpu.VMEM((2 * BLOCK, D), BF),
        pltpu.VMEM((4, 4, 4, 16, D), BF),
        pltpu.VMEM((4, 4, 4, 16, D), BF),
        pltpu.VMEM((BLOCK, INNER), BF),
        pltpu.VMEM((BLOCK, INNER), BF),
        pltpu.VMEM((BLOCK, INNER), BF),
        pltpu.VMEM((BLOCK, INNER), F32),
        pltpu.VMEM(state, BF),
        pltpu.VMEM((3,) + state, BF),
        pltpu.VMEM((2,) + state, BF),
        pltpu.VMEM((3,) + state, BF),
        pltpu.VMEM(state, F32),
        pltpu.VMEM((BLOCK, D), BF),
        pltpu.VMEM((PADBITS, BLOCK), F32),
        pltpu.VMEM((2, PADBITS, BLOCK), BF),
        pltpu.VMEM((PADBITS, 2 * BLOCK), F32),
        pltpu.VMEM((PADBITS, BLOCK), F32),
        pltpu.VMEM((UNITS, 2 * BLOCK), BF),
        pltpu.VMEM((UNITS, 2 * BLOCK), BF),
        pltpu.VMEM((UNITS, 256), F32),
        pltpu.VMEM((UNITS, 256), F32),
        pltpu.VMEM((4, 4, 4, 16, D), BF),
        pltpu.VMEM((4, 4, 4, 16, D), BF),
        pltpu.VMEM((2, 3, 3, 4, 4, 16, PART), BF),
        pltpu.VMEM((2, 3, 4, 4, 16, PART), BF),
        pltpu.VMEM((2, 3, 3, 4, 16, PART), BF),
        pltpu.VMEM((2, 3, 4, 16, PART), BF),
        pltpu.VMEM((2, 3, 3, 16, PART), BF),
        pltpu.VMEM((4, 4, PADBITS, 128), F32),
        pltpu.SemaphoreType.DMA((16,)),
        pltpu.SemaphoreType.DMA((REMOTE,)),
        pltpu.SemaphoreType.DMA((REMOTE,)),
    ]
    grad_up, grad_down, fg, pen = pl.pallas_call(
        fused,
        out_shape=(
            jax.ShapeDtypeStruct((16, D), F32),
            jax.ShapeDtypeStruct((16, D), F32),
            jax.ShapeDtypeStruct((PADBITS, BLOCK), F32),
            jax.ShapeDtypeStruct((8, 128), F32),
        ),
        in_specs=[anywhere] * 5 + [vmem] * 3 + [anywhere] * 4,
        out_specs=(vmem,) * 4,
        scratch_shapes=scratch,
        compiler_params=pltpu.CompilerParams(
            collective_id=0, has_side_effects=True, vmem_limit_bytes=60 * 1024 * 1024
        ),
    )(
        frames.reshape(BLOCK, D), w_query, w_key, w_value, w_out, wct, bias, wexp,
        w_up, w_down, decoder_stream.reshape(BLOCK, D), cotangent.reshape(BLOCK, D),
    )
    return grad_up, grad_down, fg[:BITS].T.reshape(1, BLOCK, BITS), pen[0, 0]


def solution(mesh):
    in_specs = (
        P("batch", "tm", None),
        P(),
        P(),
        P(),
        P(),
        P(),
        P(),
        P(),
        P(("tm", "batch"), None),
        P(("tm", "batch"), None),
        P("batch", "tm", None),
        P("batch", "tm", None),
    )
    out_specs = (P(("tm", "batch"), None), P(("tm", "batch"), None), P("batch", "tm", None), P())
    return jax.shard_map(body, mesh=mesh, in_specs=in_specs, out_specs=out_specs, check_vma=False)
```

time: 532 us -> 115 us (0.22)
  waiting for transfers between devices: 325 us -> 0 us
  Pallas kernels: 0 us -> 103 us
  blocking collectives: 62.9 us -> 0 us
  matrix products: 56.1 us -> 0 us
  other arithmetic: 32.1 us -> 0 us
  local copies, waits for them, and re-layouts: 36.5 us -> 10.1 us
  between operations: 17.2 us -> 0.64 us
    unnamed x5 -> x0, waiting for transfers between devices: 172 us -> none
    all_gather x3 -> x0, waiting for transfers between devices: 152 us -> none  [the longest x1 54.4 us: body(): lax.all_gather(w_down, ('tm', 'batch'), axis=0, tiled=True)]
    pallas_call x0 -> x1, Pallas kernels: none -> 103 us  [body(): pl.pallas_call(fused, out_shape=(jax.ShapeDtypeStruct((16, D), F32), jax....]
    psum x1 -> x0, blocking collectives: 62.9 us -> none  [body(): lax.psum((jnp.sum(prob, axis=0), jnp.sum(entropy)), ('tm', 'batch'))]
    dot_general x13 -> x0, matrix products: 56.1 us -> none  [the longest x3 22 us: contract_cols(): lax.dot_general(left, right, (((1,), (1,)), ((), ())), preferred_element_...]
    unnamed x34 -> x3, local copies, waits for them, and re-layouts: 33.6 us -> 3.73 us
    select_n x15 -> x0, other arithmetic: 17 us -> none  [hop(): return jnp.where(position < mine, longer, running)]
    concatenate x1 -> x0, other arithmetic: 12.4 us -> none  [body(): jnp.concatenate([contract_rows(dpre, expanded), contract_rows(act, cot_fl...]
  transfers between devices with their start and end apart: 4 -> 0, of which waited for: 4 -> 0; matrix products, arithmetic and copies ran while one was open for 11% -> 0% of each run, Pallas kernels for 0% -> 0%
where the time goes in v1:
time: 115 us; the launch traced here: 114 us
  Pallas kernels  103 us (90%)
  local copies, waits for them, and re-layouts  10.1 us (9%)
    pallas_call x1, Pallas kernels, body(): pl.pallas_call(fused, out_shape=(jax.ShapeDtypeStruct((16, D), F32), jax....  103 us
    unnamed x3, local copies, waits for them, and re-layouts  3.73 us

profile of v1, /device:TPU:0, one launch (start us, length us, event | category | flops | bytes accessed | tf_op | source)
XLA Modules:
  0.0 114.2 jit_solution(8211433521086540532)
XLA Ops:
  0.6 0.7 pad_bitcast_fusion
  1.3 0.7 copy.16.bias
  2.0 1.5 %pad.11.wct = bf16[32,1536]{1,0:T(8,128)(2,1)} pad(bf16[18,1536]{1,0:T(8,128)(2,1)} %bitcast.14, bf16[]{:T(256)} %constant.3.clone.1), padding=0_14x0_0 | pad | bytes 153602 | tf_op jit(solution)/shard_map/jit(_pad)/pad | solution.py:464
  3.5 1.5 %pad.13.wexp = bf16[32,1536]{1,0:T(8,128)(2,1)} pad(bf16[18,1536]{1,0:T(8,128)(2,1)} %param.19, bf16[]{:T(256)} %constant.3.clone.1), padding=0_14x0_0 | pad | bytes 153602 | tf_op jit(solution)/shard_map/jit(_pad)/pad | solution.py:465
  5.0 103.4 %shard_map.147 = (f32[16,1536]{1,0:T(8,128)}, f32[16,1536]{1,0:T(8,128)}, f32[32,512]{1,0:T(8,128)}, f32[8,128]{1,0:T(8,128)}) custom-call(bf16[512,1536]{1,0:T(8,128)(2,1)} %bitcast.11, bf16[1536,768]{1,0:T(8,128)(2,1)} %wq.1, bf16[1536,768]{1,0:T(8,128)(2,1)} %wk.1, bf16[1536,768]{1,0:T(8,128)(2,1)} %wv.1, bf16[768,1536]{1,0:T(8,128)(2,1)} %wo.1, ...), custom_call_target="tpu_custom_call" | custom-call | tf_op jit(solution)/shard_map/pallas_call | solution.py:510
  108.5 1.2 %slice.7 = f32[1,1]{1,0:T(1,128)} slice(f32[8,128]{1,0:T(8,128)} %get-tuple-element.11), slice={[0:1], [0:1]} | slice | bytes 8 | tf_op jit(solution)/shard_map/slice | solution.py:528
  109.7 0.8 slice_bitcast_fusion
  110.5 0.7 copy.17
  111.1 1.5 %copy.20 = f32[16,1536]{1,0:T(8,128)} copy(f32[16,1536]{1,0:T(8,128)} %get-tuple-element.20) | data formatting | bytes 196608
  112.7 1.5 %copy.21 = f32[16,1536]{1,0:T(8,128)} copy(f32[16,1536]{1,0:T(8,128)} %get-tuple-element.21) | data formatting | bytes 196608

commit v2 on v1

--- a/solution.py
+++ b/solution.py
@@ -25,7 +25,8 @@
 
 ORDER = (("x", "y", "z"), ("y", "z", "x"), ("z", "x", "y"))
 AXES = ("y", "z", "x")
-REMOTE = 130
+REMOTE = 188
+SHARE = INNER // 16
 
 
 def nn(a, b):
@@ -44,8 +45,8 @@
     frames, wq, wk, wv, wo, wct, bias, wexp, wup, wdn, stream, cot,
     gup_out, gdn_out, fg_out, pen_out,
     fr, q_w, k_w, v_w, o_w, st, ct, up, dn, q, k, v, mix,
-    own_state, a_recv, b_send, b_recv, before, hid, zt, code, dc, dc_recv,
-    act, dpre, pre_t, dact_t, gd, gu, r1, s1, r2, s2, r3, ps,
+    own_state, a_recv, prefix, history, hid, zt, code, dc, dc_recv,
+    act, dpre, pre_a, pre_b, slope, gd, gu, r1, s1, r2, s2, r3, ps,
     lsem, ssem, rsem,
 ):
     t = lax.axis_index("tm")
@@ -94,25 +95,73 @@
     def at(buf, p, fixed):
         return buf.at[tuple(fixed.get(a, slice(None)) for a in AXES) + (slice(None), cols(p))]
 
+    barrier = pltpu.get_barrier_semaphore()
+    others = [(lax.rem(t + j, 16), b) for j in range(1, 16)]
+    for device in others + [peer("x", 1), peer("x", 2), peer("x", 3), partner]:
+        pl.semaphore_signal(barrier, inc=1, device_id=device, device_id_type=MESH)
     l_fr = load(frames, fr)
     l_k = load(wk, k_w)
     l_v = load(wv, v_w)
     l_dn = load(wdn, dn.at[y, z, x])
     l_up = load(wup, up.at[y, z, x])
-    barrier = pltpu.get_barrier_semaphore()
-    for axis in AXES:
-        for step in (1, 2, 3):
-            pl.semaphore_signal(barrier, inc=1, device_id=peer(axis, step), device_id_type=MESH)
-    pl.semaphore_signal(barrier, inc=1, device_id=partner, device_id_type=MESH)
-    pl.semaphore_wait(barrier, 10)
-
-    own = {"y": y, "z": z, "x": x}
-    ag1 = []
-    for p in range(3):
-        for step in (1, 2, 3):
-            for src, buf in ((wdn, dn), (wup, up)):
-                ag1.append(send(src.at[:, cols(p)], at(buf, p, own), peer(ORDER[p][0], step)))
     l_q = load(wq, q_w)
+    pl.semaphore_wait(barrier, 19)
+
+    shards = {"up": (wup, up), "dn": (wdn, dn)}
+    ag1, ag2, ag3, ag4 = {}, {}, {}, {}
+
+    def half(buf, p, axis, n, h):
+        fixed = {a: slice(None) for a in AXES}
+        fixed[axis] = n
+        fixed[ORDER[p][0]] = pl.ds(2 * h, 2)
+        return at(buf, p, fixed)
+
+    for m in ("up", "dn"):
+        src, buf = shards[m]
+        for p in range(3):
+            ag1[m, p] = [
+                send(src.at[:, cols(p)], at(buf, p, pos), peer(ORDER[p][0], step))
+                for step in (2, 1, 3)
+            ]
+
+    def gather_second(m):
+        buf = shards[m][1]
+        for p in range(3):
+            for copy in ag1[m, p]:
+                copy.wait_recv()
+            fixed = {a: pos[a] for a in ORDER[p][1:]}
+            ag2[m, p] = [
+                send(at(buf, p, fixed), at(buf, p, fixed), peer(ORDER[p][1], step))
+                for step in (2, 1, 3)
+            ]
+
+    def gather_third(m, first):
+        buf = shards[m][1]
+        for p in range(3):
+            axis = ORDER[p][2]
+            if first:
+                for copy in ag2[m, p]:
+                    copy.wait_recv()
+            for step in (1, -1):
+                h = int((step == 1) != first)
+                mine = half(buf, p, axis, pos[axis], h)
+                ag3[m, p, step, first] = send(mine, mine, peer(axis, step))
+
+    def gather_last(m):
+        buf = shards[m][1]
+        for p in range(3):
+            axis = ORDER[p][2]
+            for step in (1, -1):
+                ag3[m, p, step, True].wait_recv()
+                block = half(buf, p, axis, shifted(axis, -step), int(step == -1))
+                ag4[m, p, step] = send(block, block, peer(axis, step))
+
+    def gather_end(m):
+        for p in range(3):
+            for step in (1, -1):
+                ag3[m, p, step, False].wait_recv()
+                ag4[m, p, step].wait_recv()
+
     l_o = load(wo, o_w)
     l_ct = load(cot, ct.at[pl.ds(0, BLOCK)])
     l_st = load(stream, st.at[pl.ds(0, BLOCK)])
@@ -133,6 +182,9 @@
     l_fr.wait()
     l_k.wait()
     project(k_w, k, None)
+    l_dn.wait()
+    l_up.wait()
+    gather_second("up")
     l_v.wait()
     project(v_w, v, None)
 
@@ -140,57 +192,21 @@
         return pl.ds(pl.multiple_of(h * HD, HD), HD)
 
     def state(h, carry):
-        own_state[h] = tn(k[:, head_cols(h)], v[:, head_cols(h)]).astype(BF)
+        rows = pl.ds(pl.multiple_of(h * HD, HD), HD)
+        own_state[rows, :] = tn(k[:, head_cols(h)], v[:, head_cols(h)]).astype(BF)
         return carry
 
     lax.fori_loop(0, HEADS, state, 0)
-    stage_a = [send(own_state, a_recv.at[step - 1], peer("y", step)) for step in (1, 2, 3)]
-
-    l_dn.wait()
-    l_up.wait()
-    for copy in ag1:
-        copy.wait_recv()
-    ag2 = []
-    for p in range(3):
-        fixed = {a: pos[a] for a in ORDER[p][1:]}
-        for step in (1, 2, 3):
-            for buf in (dn, up):
-                ag2.append(send(at(buf, p, fixed), at(buf, p, fixed), peer(ORDER[p][1], step)))
-
+
+    def share(n):
+        return pl.ds(pl.multiple_of(n * SHARE, SHARE), SHARE)
+
+    to_share = [send(own_state.at[share(d[0])], a_recv.at[t], d) for d in others]
+    a_recv[t] = own_state[share(t), :]
+    gather_second("dn")
     l_q.wait()
     project(q_w, q, 1.0 / math.sqrt(HD))
-
-    for copy in stage_a:
-        copy.wait_recv()
-
-    def combine_a(h, carry):
-        total = jnp.zeros((HD, HD), F32)
-        for step in (1, 2, 3):
-            total = total + jnp.where(y >= step, a_recv[step - 1, h].astype(F32), 0.0)
-        before[h] = total
-        b_send[0, h] = (total + own_state[h].astype(F32)).astype(BF)
-        b_send[1, h] = total.astype(BF)
-        return carry
-
-    lax.fori_loop(0, HEADS, combine_a, 0)
-    stage_b = [
-        send(b_send.at[lax.div(z + step, 4)], b_recv.at[step - 1], peer("z", step))
-        for step in (1, 2, 3)
-    ]
-
-    for copy in ag2:
-        copy.wait_recv()
-    ag3 = []
-    for p in range(3):
-        axis = ORDER[p][2]
-        mine = {axis: pos[axis]}
-        for buf in (dn, up):
-            pair = [
-                send(at(buf, p, mine), at(buf, p, mine), peer(axis, step)) for step in (1, -1)
-            ]
-            ag3.append(pair)
-
-    for r in range(2):
+    def local_rows(r):
         width = (r + 1) * 256
         keep = (
             lax.broadcasted_iota(jnp.int32, (256, width), 0) + r * 256
@@ -206,17 +222,29 @@
 
         lax.fori_loop(0, HEADS, local, 0)
 
-    for copy in stage_b:
+    local_rows(0)
+    for copy in to_share:
+        copy.wait_recv()
+    running = jnp.zeros((SHARE, HD), F32)
+    for n in range(16):
+        prefix[n] = running.astype(BF)
+        if n < 15:
+            running = running + a_recv[n].astype(F32)
+    from_share = [send(prefix.at[d[0]], history.at[share(t)], d) for d in others]
+    history[share(t), :] = prefix[t]
+
+    gather_third("up", True)
+    gather_third("up", False)
+    local_rows(1)
+    gather_third("dn", True)
+
+    for copy in from_share:
         copy.wait_recv()
     l_o.wait()
 
     def carry_in(h, carry):
-        total = before[h]
-        for step in range(3):
-            total = total + b_recv[step, h].astype(F32)
-        history = total.astype(BF)
         hc = head_cols(h)
-        m = mix[:, hc] + nn(q[:, hc], history)
+        m = mix[:, hc] + nn(q[:, hc], history[hc, :])
         meansq = jnp.mean(m * m, axis=-1, keepdims=True)
         q[:, hc] = (m * lax.rsqrt(meansq + EPSILON)).astype(BF)
         return carry
@@ -234,18 +262,8 @@
     code[0] = jnp.tanh(zvals).astype(BF)
     x_code = send(code.at[0], code.at[1], partner)
 
-    ag4 = []
-    for p in range(3):
-        axis = ORDER[p][2]
-        pair_dn, pair_up = ag3[2 * p], ag3[2 * p + 1]
-        pair_dn[0].wait_recv()
-        left = {axis: shifted(axis, -1)}
-        ag4.append(send(at(dn, p, left), at(dn, p, left), peer(axis, 1)))
-        pair_up[1].wait_recv()
-        right = {axis: shifted(axis, 1)}
-        ag4.append(send(at(up, p, right), at(up, p, right), peer(axis, -1)))
-        pair_dn[1].wait_recv()
-        pair_up[0].wait_recv()
+    gather_last("up")
+    gather_third("dn", False)
 
     def sums(slot):
         zv = zt[...]
@@ -281,7 +299,7 @@
     expand(0)
     x_code.wait_recv()
     expand(1)
-    x_ct.wait_recv()
+    gather_last("dn")
 
     def ps_send(stage, axis, value):
         ps[stage, pos[axis]] = value
@@ -296,37 +314,42 @@
     p_core.wait_recv()
     p_x = ps_send(1, "x", ps[0, 0] + ps[0, 1])
 
-    for copy in ag4:
-        copy.wait_recv()
+    gather_end("up")
 
     up_all = up.reshape(UNITS, D)
     dn_all = dn.reshape(UNITS, D)
-    back = nt(wexp[...], up_all[...]).astype(BF)
+    tiles = [pl.ds(i * 256, 256) for i in range(4)]
     coeff = math.sqrt(2.0 / math.pi)
-
-    def forward(i, carry):
-        tok = pl.multiple_of(i * 256, 256)
-        rows = pl.ds(tok, 256)
-        pre_t[...] = nt(up_all[...], st[rows, :])
-        dact_t[...] = nt(dn_all[...], ct[rows, :])
-
-        def slab(j, inner):
-            us = pl.ds(pl.multiple_of(j * 64, 64), 64)
-            val = pre_t[us, :]
+    buffers = (pre_a, pre_b)
+
+    def act_slabs(rows, pre):
+        for j in range(UNITS // 64):
+            us = pl.ds(j * 64, 64)
+            val = pre[us, :]
             square = val * val
-            half = 0.5 * jnp.tanh(val * (square * (coeff * 0.044715) + coeff)) + 0.5
-            gelu = val * half
-            slope = half + gelu * (1.0 - half) * (square * (6.0 * 0.044715 * coeff) + 2.0 * coeff)
+            half_t = 0.5 * jnp.tanh(val * (square * (coeff * 0.044715) + coeff)) + 0.5
+            gelu = val * half_t
             act[us, rows] = gelu.astype(BF)
-            dpre[us, rows] = (dact_t[us, :] * slope).astype(BF)
-            return inner
-
-        lax.fori_loop(0, UNITS // 64, slab, 0)
-        dc[:, rows] = nn(back, dpre[:, rows])
-        return carry
-
-    lax.fori_loop(0, 4, forward, 0)
-    x_dc = send(dc.at[:, pl.ds(BLOCK, BLOCK)], dc_recv, partner)
+            slope[us, rows] = half_t + gelu * (1.0 - half_t) * (
+                square * (6.0 * 0.044715 * coeff) + 2.0 * coeff
+            )
+
+    for i in range(5):
+        if i < 4:
+            buffers[i % 2][...] = nt(up_all[...], st[tiles[i], :])
+        if i > 0:
+            act_slabs(tiles[i - 1], buffers[(i - 1) % 2])
+
+    def dpre_all():
+        for i in range(5):
+            if i < 4:
+                buffers[i % 2][...] = nt(dn_all[...], ct[tiles[i], :])
+            if i > 0:
+                for j in range(UNITS // 64):
+                    us = pl.ds(j * 64, 64)
+                    dpre[us, tiles[i - 1]] = (
+                        buffers[(i - 1) % 2][us, :] * slope[us, tiles[i - 1]]
+                    ).astype(BF)
 
     gd_all = gd.reshape(UNITS, D)
     gu_all = gu.reshape(UNITS, D)
@@ -340,90 +363,119 @@
         lax.fori_loop(0, PART // 256, tile, 0)
 
     grads = (gd, gu)
-    way = (1, -1)
-    far, near, joined = {}, {}, {}
+    far, plain, joined, second, third = {}, {}, {}, {}, {}
+
+    def landing(m, p, slot, h):
+        if p == 0:
+            return r1.at[m, p, slot, :, pl.ds(2 * h, 2)]
+        return r1.at[m, p, slot, pl.ds(2 * h, 2)] if p == 1 else r1.at[m, p, slot, pl.ds(2 * h, 2)]
 
     def first_sends(m, p):
         axis = ORDER[p][2]
-        s = way[m]
-        far[m, p] = send(
-            at(grads[m], p, {axis: shifted(axis, 2)}), r1.at[m, p, 0], peer(axis, s)
-        )
-        near[m, p] = send(
-            at(grads[m], p, {axis: shifted(axis, -s)}), r1.at[m, p, 1], peer(axis, -s)
-        )
+        for step in (1, -1):
+            h = int(step == -1)
+            far[m, p, step] = send(
+                half(grads[m], p, axis, shifted(axis, 2), h), landing(m, p, 0, h), peer(axis, step)
+            )
+        for step in (1, -1):
+            h = int(step == 1)
+            slot = 1 if step == 1 else 2
+            plain[m, p, step] = send(
+                half(grads[m], p, axis, shifted(axis, step), h),
+                landing(m, p, slot, h),
+                peer(axis, step),
+            )
 
     def forward_sum(m, p):
         axis = ORDER[p][2]
-        s = way[m]
-        far[m, p].wait_recv()
-        block = at(grads[m], p, {axis: shifted(axis, s)})
-
-        def add(i, carry):
-            block[i] = (block[i].astype(F32) + r1[m, p, 0, i].astype(F32)).astype(BF)
+        for step in (1, -1):
+            h = int(step == -1)
+            slot = 1 if step == 1 else 2
+            far[m, p, step].wait_recv()
+            block = half(grads[m], p, axis, shifted(axis, step), h)
+            came = landing(m, p, 0, h)
+            block[...] = (block[...].astype(F32) + came[...].astype(F32)).astype(BF)
+            joined[m, p, step] = send(block, landing(m, p, slot, h), peer(axis, step))
+
+    def second_sends(m, p):
+        axis = ORDER[p][2]
+        for step in (1, -1):
+            plain[m, p, step].wait_recv()
+            joined[m, p, step].wait_recv()
+        block = at(grads[m], p, {axis: pos[axis]})
+
+        def total1(i, carry):
+            s1[m, p, i] = (
+                block[i].astype(F32)
+                + r1[m, p, 1, i].astype(F32)
+                + r1[m, p, 2, i].astype(F32)
+            ).astype(BF)
             return carry
 
-        lax.fori_loop(0, 4, add, 0)
-        joined[m, p] = send(block, r1.at[m, p, 2], peer(axis, s))
-
+        lax.fori_loop(0, 4, total1, 0)
+        axis = ORDER[p][1]
+        for step in (2, 1, 3):
+            n = shifted(axis, step)
+            src = s1.at[m, p, n] if p == 0 else s1.at[m, p, :, n]
+            second[m, p, step] = send(src, r2.at[m, p, step - 1], peer(axis, step))
+
+    def third_sends(m, p):
+        axis = ORDER[p][1]
+        for step in (1, 2, 3):
+            second[m, p, step].wait_recv()
+        mine = s1.at[m, p, pos[axis]] if p == 0 else s1.at[m, p, :, pos[axis]]
+        total = mine[...].astype(F32)
+        for step in range(3):
+            total = total + r2[m, p, step].astype(F32)
+        s2[m, p] = total.astype(BF)
+        axis = ORDER[p][0]
+        for step in (2, 1, 3):
+            third[m, p, step] = send(
+                s2.at[m, p, shifted(axis, step)], r3.at[m, p, step - 1], peer(axis, step)
+            )
+
+    scale = 1.0 / math.sqrt(TOTAL)
+
+    def last_sum(m, p):
+        out = (gdn_out, gup_out)[m]
+        axis = ORDER[p][0]
+        total = s2[m, p, pos[axis]].astype(F32)
+        for step in (1, 2, 3):
+            third[m, p, step].wait_recv()
+            total = total + r3[m, p, step - 1].astype(F32)
+        out[:, cols(p)] = total * scale
+
+    x_ct.wait_recv()
     for p in range(3):
         gradient(act, ct, gd_all, p)
         first_sends(0, p)
+    gather_end("dn")
+    dpre_all()
+    for p in range(3):
+        forward_sum(0, p)
     for p in range(3):
         gradient(dpre, st, gu_all, p)
         first_sends(1, p)
-        forward_sum(0, p)
-
     for copy in p_x:
         copy.wait_recv()
     p_y = ps_send(2, "y", ps_sum(1))
-
-    for p in range(3):
-        forward_sum(1, p)
-
-    second = {}
-    for m in range(2):
-        for p in range(3):
-            axis = ORDER[p][2]
-            near[m, p].wait_recv()
-            joined[m, p].wait_recv()
-            block = at(grads[m], p, {axis: pos[axis]})
-
-            def total1(i, carry):
-                s1[m, p, i] = (
-                    block[i].astype(F32)
-                    + r1[m, p, 1, i].astype(F32)
-                    + r1[m, p, 2, i].astype(F32)
-                ).astype(BF)
-                return carry
-
-            lax.fori_loop(0, 4, total1, 0)
-            axis = ORDER[p][1]
-            for step in (1, 2, 3):
-                n = shifted(axis, step)
-                src = s1.at[m, p, n] if p == 0 else s1.at[m, p, :, n]
-                second[m, p, step] = send(src, r2.at[m, p, step - 1], peer(axis, step))
-
+    back = nt(wexp[...], up_all[...]).astype(BF)
+
+    for i in range(4):
+        dc[:, tiles[i]] = nn(back, dpre[:, tiles[i]])
+    x_dc = send(dc.at[:, pl.ds(BLOCK, BLOCK)], dc_recv, partner)
     for copy in p_y:
         copy.wait_recv()
     p_z = ps_send(3, "z", ps_sum(2))
 
-    third = {}
-    for m in range(2):
-        for p in range(3):
-            axis = ORDER[p][1]
-            for step in (1, 2, 3):
-                second[m, p, step].wait_recv()
-            mine = s1.at[m, p, pos[axis]] if p == 0 else s1.at[m, p, :, pos[axis]]
-            total = mine[...].astype(F32)
-            for step in range(3):
-                total = total + r2[m, p, step].astype(F32)
-            s2[m, p] = total.astype(BF)
-            axis = ORDER[p][0]
-            for step in (1, 2, 3):
-                third[m, p, step] = send(
-                    s2.at[m, p, shifted(axis, step)], r3.at[m, p, step - 1], peer(axis, step)
-                )
+    for p in range(3):
+        second_sends(0, p)
+    for p in range(3):
+        forward_sum(1, p)
+    for p in range(3):
+        third_sends(0, p)
+    for p in range(3):
+        second_sends(1, p)
 
     for copy in p_z:
         copy.wait_recv()
@@ -443,15 +495,12 @@
         -2.0 * zv - lq[:, :1] + lp[:, :1]
     )
 
-    scale = 1.0 / math.sqrt(TOTAL)
-    for m, out in ((0, gdn_out), (1, gup_out)):
-        for p in range(3):
-            axis = ORDER[p][0]
-            total = s2[m, p, pos[axis]].astype(F32)
-            for step in (1, 2, 3):
-                third[m, p, step].wait_recv()
-                total = total + r3[m, p, step - 1].astype(F32)
-            out[:, cols(p)] = total * scale
+    for p in range(3):
+        last_sum(0, p)
+    for p in range(3):
+        third_sends(1, p)
+    for p in range(3):
+        last_sum(1, p)
     for copy in sent:
         copy.wait_send()
 
@@ -466,7 +515,6 @@
     bias = jnp.pad(code_bias, (0, spare)).reshape(PADBITS, 1)
     anywhere = pl.BlockSpec(memory_space=pl.ANY)
     vmem = pl.BlockSpec(memory_space=pltpu.VMEM)
-    state = (HEADS, HD, HD)
     scratch = [
         pltpu.VMEM((BLOCK, D), BF),
         pltpu.VMEM((D, INNER), BF),
@@ -481,11 +529,10 @@
         pltpu.VMEM((BLOCK, INNER), BF),
         pltpu.VMEM((BLOCK, INNER), BF),
         pltpu.VMEM((BLOCK, INNER), F32),
-        pltpu.VMEM(state, BF),
-        pltpu.VMEM((3,) + state, BF),
-        pltpu.VMEM((2,) + state, BF),
-        pltpu.VMEM((3,) + state, BF),
-        pltpu.VMEM(state, F32),
+        pltpu.VMEM((INNER, HD), BF),
+        pltpu.VMEM((16, SHARE, HD), BF),
+        pltpu.VMEM((16, SHARE, HD), BF),
+        pltpu.VMEM((INNER, HD), BF),
         pltpu.VMEM((BLOCK, D), BF),
         pltpu.VMEM((PADBITS, BLOCK), F32),
         pltpu.VMEM((2, PADBITS, BLOCK), BF),
@@ -495,6 +542,7 @@
         pltpu.VMEM((UNITS, 2 * BLOCK), BF),
         pltpu.VMEM((UNITS, 256), F32),
         pltpu.VMEM((UNITS, 256), F32),
+        pltpu.VMEM((UNITS, 2 * BLOCK), F32),
         pltpu.VMEM((4, 4, 4, 16, D), BF),
         pltpu.VMEM((4, 4, 4, 16, D), BF),
         pltpu.VMEM((2, 3, 3, 4, 4, 16, PART), BF),

time: 115 us -> 95.8 us (0.83)
  Pallas kernels: 103 us -> 84.6 us
    pallas_call x1, Pallas kernels: 103 us -> 84.6 us  [body(): pl.pallas_call(fused, out_shape=(jax.ShapeDtypeStruct((16, D), F32), jax....]
where the time goes in v2:
time: 95.8 us; the launch traced here: 95.4 us
  Pallas kernels  84.6 us (88%)
  local copies, waits for them, and re-layouts  10.1 us (11%)
    pallas_call x1, Pallas kernels, body(): pl.pallas_call(fused, out_shape=(jax.ShapeDtypeStruct((16, D), F32), jax....  84.6 us
    unnamed x3, local copies, waits for them, and re-layouts  3.73 us

profile of v2, /device:TPU:0, one launch (start us, length us, event | category | flops | bytes accessed | tf_op | source)
XLA Modules:
  0.0 95.4 jit_solution(17296438026570679746)
XLA Ops:
  0.6 0.7 pad_bitcast_fusion
  1.3 0.7 copy.16.bias
  2.0 1.5 %pad.11.wct = bf16[32,1536]{1,0:T(8,128)(2,1)} pad(bf16[18,1536]{1,0:T(8,128)(2,1)} %bitcast.14, bf16[]{:T(256)} %constant.3.clone.1), padding=0_14x0_0 | pad | bytes 153602 | tf_op jit(solution)/shard_map/jit(_pad)/pad | solution.py:513
  3.5 1.5 %pad.13.wexp = bf16[32,1536]{1,0:T(8,128)(2,1)} pad(bf16[18,1536]{1,0:T(8,128)(2,1)} %param.19, bf16[]{:T(256)} %constant.3.clone.1), padding=0_14x0_0 | pad | bytes 153602 | tf_op jit(solution)/shard_map/jit(_pad)/pad | solution.py:514
  5.0 84.6 %shard_map.147 = (f32[16,1536]{1,0:T(8,128)}, f32[16,1536]{1,0:T(8,128)}, f32[32,512]{1,0:T(8,128)}, f32[8,128]{1,0:T(8,128)}) custom-call(bf16[512,1536]{1,0:T(8,128)(2,1)} %bitcast.11, bf16[1536,768]{1,0:T(8,128)(2,1)} %wq.1, bf16[1536,768]{1,0:T(8,128)(2,1)} %wk.1, bf16[1536,768]{1,0:T(8,128)(2,1)} %wv.1, bf16[768,1536]{1,0:T(8,128)(2,1)} %wo.1, ...), custom_call_target="tpu_custom_call" | custom-call | tf_op jit(solution)/shard_map/pallas_call | solution.py:558
  89.7 1.2 %slice.7 = f32[1,1]{1,0:T(1,128)} slice(f32[8,128]{1,0:T(8,128)} %get-tuple-element.11), slice={[0:1], [0:1]} | slice | bytes 8 | tf_op jit(solution)/shard_map/slice | solution.py:576
  90.9 0.8 slice_bitcast_fusion
  91.7 0.7 copy.17
  92.4 1.5 %copy.20 = f32[16,1536]{1,0:T(8,128)} copy(f32[16,1536]{1,0:T(8,128)} %get-tuple-element.20) | data formatting | bytes 196608
  93.9 1.5 %copy.21 = f32[16,1536]{1,0:T(8,128)} copy(f32[16,1536]{1,0:T(8,128)} %get-tuple-element.21) | data formatting | bytes 196608

commit v3 on v2

--- a/solution.py
+++ b/solution.py
@@ -25,7 +25,8 @@
 
 ORDER = (("x", "y", "z"), ("y", "z", "x"), ("z", "x", "y"))
 AXES = ("y", "z", "x")
-REMOTE = 188
+ARRIVALS = 58
+DEPARTURES = 17
 SHARE = INNER // 16
 
 
@@ -42,11 +43,11 @@
 
 
 def fused(
-    frames, wq, wk, wv, wo, wct, bias, wexp, wup, wdn, stream, cot,
-    gup_out, gdn_out, fg_out, pen_out,
+    frames, wq, wk, wv, wo, w_code, bias, w_exp, wup, wdn, stream, cot,
+    grad_out, fg_out, pen_out,
     fr, q_w, k_w, v_w, o_w, st, ct, up, dn, q, k, v, mix,
     own_state, a_recv, prefix, history, hid, zt, code, dc, dc_recv,
-    act, dpre, pre_a, pre_b, slope, gd, gu, r1, s1, r2, s2, r3, ps,
+    wexp, act, dpre, pre_a, pre_b, slope, gd, gu, r1, s1, r2, s2, r3, ps,
     lsem, ssem, rsem,
 ):
     t = lax.axis_index("tm")
@@ -67,19 +68,33 @@
         return (y * 4 + n, b)
 
     partner = (t, x * 2 + 1 - c)
-    count = [0]
-    sent = []
-
-    def send(src, dst, device):
-        i = count[0]
-        count[0] += 1
-        copy = pltpu.make_async_remote_copy(
-            src_ref=src, dst_ref=dst, send_sem=ssem.at[i], recv_sem=rsem.at[i],
+    arrivals, departures = {}, {}
+
+    def semaphores(arrival, departure):
+        return (
+            ssem.at[departures.setdefault(departure, len(departures))],
+            rsem.at[arrivals.setdefault(arrival, len(arrivals))],
+        )
+
+    def send(src, dst, device, arrival, departure):
+        out, into = semaphores(arrival, departure)
+        pltpu.make_async_remote_copy(
+            src_ref=src, dst_ref=dst, send_sem=out, recv_sem=into,
             device_id=device, device_id_type=MESH,
+        ).start()
+
+    def waiter(arrival, departure, size):
+        out, into = semaphores(arrival, departure)
+        return pltpu.make_async_remote_copy(
+            src_ref=size, dst_ref=size, send_sem=out, recv_sem=into,
+            device_id=partner, device_id_type=MESH,
         )
-        copy.start()
-        sent.append(copy)
-        return copy
+
+    def arrived(arrival, size):
+        waiter(arrival, "ag1", size).wait_recv()
+
+    def departed(departure, size):
+        waiter("a1", departure, size).wait_send()
 
     loads = [0]
 
@@ -97,7 +112,7 @@
 
     barrier = pltpu.get_barrier_semaphore()
     others = [(lax.rem(t + j, 16), b) for j in range(1, 16)]
-    for device in others + [peer("x", 1), peer("x", 2), peer("x", 3), partner]:
+    for device in [peer(axis, step) for axis in AXES for step in (1, 2, 3)] + [partner]:
         pl.semaphore_signal(barrier, inc=1, device_id=device, device_id_type=MESH)
     l_fr = load(frames, fr)
     l_k = load(wk, k_w)
@@ -105,10 +120,16 @@
     l_dn = load(wdn, dn.at[y, z, x])
     l_up = load(wup, up.at[y, z, x])
     l_q = load(wq, q_w)
-    pl.semaphore_wait(barrier, 19)
+    wexp[...] = jnp.zeros_like(wexp)
+    wexp[pl.ds(0, BITS), :] = w_exp[...]
+    bit = lax.broadcasted_iota(jnp.int32, (PADBITS, BLOCK), 0)
+    offset = jnp.zeros((PADBITS, BLOCK), F32)
+    for i in range(BITS):
+        offset = jnp.where(bit == i, bias[i], offset)
+    zt[...] = offset
+    pl.semaphore_wait(barrier, 10)
 
     shards = {"up": (wup, up), "dn": (wdn, dn)}
-    ag1, ag2, ag3, ag4 = {}, {}, {}, {}
 
     def half(buf, p, axis, n, h):
         fixed = {a: slice(None) for a in AXES}
@@ -119,54 +140,48 @@
     for m in ("up", "dn"):
         src, buf = shards[m]
         for p in range(3):
-            ag1[m, p] = [
-                send(src.at[:, cols(p)], at(buf, p, pos), peer(ORDER[p][0], step))
-                for step in (2, 1, 3)
-            ]
+            for step in (2, 1, 3):
+                dst = at(buf, p, pos)
+                send(src.at[:, cols(p)], dst, peer(ORDER[p][0], step), ("ag1", m, p), "ag1")
 
     def gather_second(m):
         buf = shards[m][1]
         for p in range(3):
-            for copy in ag1[m, p]:
-                copy.wait_recv()
-            fixed = {a: pos[a] for a in ORDER[p][1:]}
-            ag2[m, p] = [
-                send(at(buf, p, fixed), at(buf, p, fixed), peer(ORDER[p][1], step))
-                for step in (2, 1, 3)
-            ]
+            arrived(("ag1", m, p), r3.at[0, 0])
+            line = at(buf, p, {a: pos[a] for a in ORDER[p][1:]})
+            for step in (2, 1, 3):
+                send(line, line, peer(ORDER[p][1], step), ("ag2", m, p), "ag2")
 
     def gather_third(m, first):
         buf = shards[m][1]
         for p in range(3):
             axis = ORDER[p][2]
             if first:
-                for copy in ag2[m, p]:
-                    copy.wait_recv()
+                arrived(("ag2", m, p), r2.at[0, 0])
             for step in (1, -1):
                 h = int((step == 1) != first)
                 mine = half(buf, p, axis, pos[axis], h)
-                ag3[m, p, step, first] = send(mine, mine, peer(axis, step))
+                send(mine, mine, peer(axis, step), ("ag3", m, p, first), ("ag3", m))
 
     def gather_last(m):
         buf = shards[m][1]
         for p in range(3):
             axis = ORDER[p][2]
+            arrived(("ag3", m, p, True), r1.at[0, 0, 0])
             for step in (1, -1):
-                ag3[m, p, step, True].wait_recv()
                 block = half(buf, p, axis, shifted(axis, -step), int(step == -1))
-                ag4[m, p, step] = send(block, block, peer(axis, step))
+                send(block, block, peer(axis, step), ("ag3", m, p, False), ("ag3", m))
 
     def gather_end(m):
         for p in range(3):
-            for step in (1, -1):
-                ag3[m, p, step, False].wait_recv()
-                ag4[m, p, step].wait_recv()
+            arrived(("ag3", m, p, False), r1.at[0, 0, pl.ds(0, 2)])
 
     l_o = load(wo, o_w)
     l_ct = load(cot, ct.at[pl.ds(0, BLOCK)])
     l_st = load(stream, st.at[pl.ds(0, BLOCK)])
-    x_ct = send(cot, ct.at[pl.ds(BLOCK, BLOCK)], partner)
-    x_st = send(stream, st.at[pl.ds(BLOCK, BLOCK)], partner)
+    there = pl.ds(BLOCK, BLOCK)
+    send(stream, st.at[there], partner, "stream", "tokens")
+    send(cot, ct.at[there], partner, "cot", "tokens")
 
     def project(weights, out, scale):
         def tile(i, carry):
@@ -201,7 +216,8 @@
     def share(n):
         return pl.ds(pl.multiple_of(n * SHARE, SHARE), SHARE)
 
-    to_share = [send(own_state.at[share(d[0])], a_recv.at[t], d) for d in others]
+    for d in others:
+        send(own_state.at[share(d[0])], a_recv.at[t], d, "a1", "a1")
     a_recv[t] = own_state[share(t), :]
     gather_second("dn")
     l_q.wait()
@@ -223,14 +239,14 @@
         lax.fori_loop(0, HEADS, local, 0)
 
     local_rows(0)
-    for copy in to_share:
-        copy.wait_recv()
+    arrived("a1", prefix.at[pl.ds(0, 15)])
     running = jnp.zeros((SHARE, HD), F32)
     for n in range(16):
         prefix[n] = running.astype(BF)
         if n < 15:
             running = running + a_recv[n].astype(F32)
-    from_share = [send(prefix.at[d[0]], history.at[share(t)], d) for d in others]
+    for d in others:
+        send(prefix.at[d[0]], history.at[share(t)], d, "a2", "a2")
     history[share(t), :] = prefix[t]
 
     gather_third("up", True)
@@ -238,8 +254,7 @@
     local_rows(1)
     gather_third("dn", True)
 
-    for copy in from_share:
-        copy.wait_recv()
+    arrived("a2", prefix.at[pl.ds(0, 15)])
     l_o.wait()
 
     def carry_in(h, carry):
@@ -257,10 +272,10 @@
         return carry
 
     lax.fori_loop(0, 2, out_tile, 0)
-    zvals = nt(wct[...], hid[...]) + bias[...]
-    zt[...] = zvals
+    zt[pl.ds(0, BITS), :] += nt(w_code[...], hid[...])
+    zvals = zt[...]
     code[0] = jnp.tanh(zvals).astype(BF)
-    x_code = send(code.at[0], code.at[1], partner)
+    send(code.at[0], code.at[1], partner, "code", "code")
 
     gather_last("up")
     gather_third("dn", False)
@@ -280,11 +295,11 @@
         ps[0, slot] = jnp.broadcast_to(tile, (PADBITS, 128))
 
     sums(c)
-    p_core = send(ps.at[0, c], ps.at[0, c], partner)
+    send(ps.at[0, c], ps.at[0, c], partner, ("ps", 0), ("ps", 0))
 
     l_ct.wait()
     l_st.wait()
-    x_st.wait_recv()
+    arrived("stream", st.at[there])
 
     def expand(slot):
         def tile(i, carry):
@@ -297,22 +312,22 @@
         lax.fori_loop(0, 2, tile, 0)
 
     expand(0)
-    x_code.wait_recv()
+    arrived("code", code.at[1])
     expand(1)
     gather_last("dn")
 
     def ps_send(stage, axis, value):
         ps[stage, pos[axis]] = value
-        return [
-            send(ps.at[stage, pos[axis]], ps.at[stage, pos[axis]], peer(axis, step))
-            for step in (1, 2, 3)
-        ]
+        mine = ps.at[stage, pos[axis]]
+        for step in (1, 2, 3):
+            send(mine, mine, peer(axis, step), ("ps", stage), ("ps", stage))
 
     def ps_sum(stage):
+        arrived(("ps", stage), ps.at[stage, pl.ds(0, 3)])
         return ps[stage, 0] + ps[stage, 1] + ps[stage, 2] + ps[stage, 3]
 
-    p_core.wait_recv()
-    p_x = ps_send(1, "x", ps[0, 0] + ps[0, 1])
+    arrived(("ps", 0), ps.at[0, 0])
+    ps_send(1, "x", ps[0, 0] + ps[0, 1])
 
     gather_end("up")
 
@@ -363,7 +378,6 @@
         lax.fori_loop(0, PART // 256, tile, 0)
 
     grads = (gd, gu)
-    far, plain, joined, second, third = {}, {}, {}, {}, {}
 
     def landing(m, p, slot, h):
         if p == 0:
@@ -374,34 +388,28 @@
         axis = ORDER[p][2]
         for step in (1, -1):
             h = int(step == -1)
-            far[m, p, step] = send(
-                half(grads[m], p, axis, shifted(axis, 2), h), landing(m, p, 0, h), peer(axis, step)
-            )
+            block = half(grads[m], p, axis, shifted(axis, 2), h)
+            send(block, landing(m, p, 0, h), peer(axis, step), ("far", m, p), ("rs1", m))
         for step in (1, -1):
             h = int(step == 1)
             slot = 1 if step == 1 else 2
-            plain[m, p, step] = send(
-                half(grads[m], p, axis, shifted(axis, step), h),
-                landing(m, p, slot, h),
-                peer(axis, step),
-            )
+            block = half(grads[m], p, axis, shifted(axis, step), h)
+            send(block, landing(m, p, slot, h), peer(axis, step), ("near", m, p), ("rs1", m))
 
     def forward_sum(m, p):
         axis = ORDER[p][2]
+        arrived(("far", m, p), r1.at[m, p, 0])
         for step in (1, -1):
             h = int(step == -1)
             slot = 1 if step == 1 else 2
-            far[m, p, step].wait_recv()
             block = half(grads[m], p, axis, shifted(axis, step), h)
             came = landing(m, p, 0, h)
             block[...] = (block[...].astype(F32) + came[...].astype(F32)).astype(BF)
-            joined[m, p, step] = send(block, landing(m, p, slot, h), peer(axis, step))
+            send(block, landing(m, p, slot, h), peer(axis, step), ("near", m, p), ("rs1", m))
 
     def second_sends(m, p):
         axis = ORDER[p][2]
-        for step in (1, -1):
-            plain[m, p, step].wait_recv()
-            joined[m, p, step].wait_recv()
+        arrived(("near", m, p), r1.at[m, p, pl.ds(1, 2)])
         block = at(grads[m], p, {axis: pos[axis]})
 
         def total1(i, carry):
@@ -417,12 +425,11 @@
         for step in (2, 1, 3):
             n = shifted(axis, step)
             src = s1.at[m, p, n] if p == 0 else s1.at[m, p, :, n]
-            second[m, p, step] = send(src, r2.at[m, p, step - 1], peer(axis, step))
+            send(src, r2.at[m, p, step - 1], peer(axis, step), ("rs2", m, p), "rs2")
 
     def third_sends(m, p):
         axis = ORDER[p][1]
-        for step in (1, 2, 3):
-            second[m, p, step].wait_recv()
+        arrived(("rs2", m, p), r2.at[m, p])
         mine = s1.at[m, p, pos[axis]] if p == 0 else s1.at[m, p, :, pos[axis]]
         total = mine[...].astype(F32)
         for step in range(3):
@@ -430,22 +437,20 @@
         s2[m, p] = total.astype(BF)
         axis = ORDER[p][0]
         for step in (2, 1, 3):
-            third[m, p, step] = send(
-                s2.at[m, p, shifted(axis, step)], r3.at[m, p, step - 1], peer(axis, step)
-            )
+            src = s2.at[m, p, shifted(axis, step)]
+            send(src, r3.at[m, p, step - 1], peer(axis, step), ("rs3", m, p), "rs3")
 
     scale = 1.0 / math.sqrt(TOTAL)
 
     def last_sum(m, p):
-        out = (gdn_out, gup_out)[m]
         axis = ORDER[p][0]
         total = s2[m, p, pos[axis]].astype(F32)
-        for step in (1, 2, 3):
-            third[m, p, step].wait_recv()
-            total = total + r3[m, p, step - 1].astype(F32)
-        out[:, cols(p)] = total * scale
-
-    x_ct.wait_recv()
+        arrived(("rs3", m, p), r3.at[m, p])
+        for step in range(3):
+            total = total + r3[m, p, step].astype(F32)
+        grad_out[pl.ds(16 * (1 - m), 16), cols(p)] = total * scale
+
+    arrived("cot", ct.at[there])
     for p in range(3):
         gradient(act, ct, gd_all, p)
         first_sends(0, p)
@@ -456,17 +461,13 @@
     for p in range(3):
         gradient(dpre, st, gu_all, p)
         first_sends(1, p)
-    for copy in p_x:
-        copy.wait_recv()
-    p_y = ps_send(2, "y", ps_sum(1))
+    ps_send(2, "y", ps_sum(1))
     back = nt(wexp[...], up_all[...]).astype(BF)
 
     for i in range(4):
         dc[:, tiles[i]] = nn(back, dpre[:, tiles[i]])
-    x_dc = send(dc.at[:, pl.ds(BLOCK, BLOCK)], dc_recv, partner)
-    for copy in p_y:
-        copy.wait_recv()
-    p_z = ps_send(3, "z", ps_sum(2))
+    send(dc.at[:, there], dc_recv, partner, "dc", "dc")
+    ps_send(3, "z", ps_sum(2))
 
     for p in range(3):
         second_sends(0, p)
@@ -477,23 +478,23 @@
     for p in range(3):
         second_sends(1, p)
 
-    for copy in p_z:
-        copy.wait_recv()
-    x_dc.wait_recv()
+    arrived("dc", dc_recv)
     sums_all = ps_sum(3)
     row = lax.broadcasted_iota(jnp.int32, (PADBITS, 128), 0)
     pbar = jnp.where(row < BITS, sums_all / TOTAL, 0.5)
     lp, lq = jnp.log(pbar), jnp.log(1.0 - pbar)
     spread = jnp.where(row < BITS, -(pbar * lp + (1.0 - pbar) * lq), 0.0)
     batch_ent = jnp.sum(spread, axis=0, keepdims=True)
-    pen_out[...] = jnp.broadcast_to(sums_all[24:25, :] / TOTAL - batch_ent, (8, 128))
+    pen_out[...] = (sums_all[24:25, :] / TOTAL - batch_ent)[:, :1]
     zv = zt[...]
     smooth = jnp.tanh(zv)
     prob = jax.nn.sigmoid(2.0 * zv)
     dcodes = nt(wexp[...], ct[pl.ds(0, BLOCK), :]) + dc[:, pl.ds(0, BLOCK)] + dc_recv[...]
-    fg_out[...] = dcodes * (1.0 - smooth * smooth) + ENT_WEIGHT * 2.0 * prob * (1.0 - prob) * (
+    fg = dcodes * (1.0 - smooth * smooth) + ENT_WEIGHT * 2.0 * prob * (1.0 - prob) * (
         -2.0 * zv - lq[:, :1] + lp[:, :1]
     )
+    for i in range(BITS):
+        fg_out[i] = fg[i : i + 1, :]
 
     for p in range(3):
         last_sum(0, p)
@@ -501,19 +502,23 @@
         third_sends(1, p)
     for p in range(3):
         last_sum(1, p)
-    for copy in sent:
-        copy.wait_send()
+    for departure, size in (
+        ("ag1", r3), ("ag2", r2), (("ag3", "up"), r1.at[0]), (("ag3", "dn"), r1.at[0]),
+        ("tokens", ct), ("a1", prefix.at[pl.ds(0, 15)]), ("a2", prefix.at[pl.ds(0, 15)]),
+        ("code", code.at[0]), (("ps", 0), ps.at[0, 0]), (("ps", 1), ps.at[1, pl.ds(0, 3)]),
+        (("ps", 2), ps.at[2, pl.ds(0, 3)]), (("ps", 3), ps.at[3, pl.ds(0, 3)]), ("dc", dc_recv),
+        (("rs1", 0), r1.at[0]), (("rs1", 1), r1.at[1]), ("rs2", r2), ("rs3", r3),
+    ):
+        departed(departure, size)
+    assert (len(arrivals), len(departures)) == (ARRIVALS, DEPARTURES), (len(arrivals), len(departures))
 
 
 def body(
     frames, w_query, w_key, w_value, w_out, w_code, code_bias, w_expand, w_up, w_down,
     decoder_stream, cotangent,
 ):
-    spare = PADBITS - BITS
-    wct = jnp.pad(w_code.T, ((0, spare), (0, 0)))
-    wexp = jnp.pad(w_expand, ((0, spare), (0, 0)))
-    bias = jnp.pad(code_bias, (0, spare)).reshape(PADBITS, 1)
     anywhere = pl.BlockSpec(memory_space=pl.ANY)
+    smem = pl.BlockSpec(memory_space=pltpu.SMEM)
     vmem = pl.BlockSpec(memory_space=pltpu.VMEM)
     scratch = [
         pltpu.VMEM((BLOCK, D), BF),
@@ -538,6 +543,7 @@
         pltpu.VMEM((2, PADBITS, BLOCK), BF),
         pltpu.VMEM((PADBITS, 2 * BLOCK), F32),
         pltpu.VMEM((PADBITS, BLOCK), F32),
+        pltpu.VMEM((PADBITS, D), BF),
         pltpu.VMEM((UNITS, 2 * BLOCK), BF),
         pltpu.VMEM((UNITS, 2 * BLOCK), BF),
         pltpu.VMEM((UNITS, 256), F32),
@@ -552,28 +558,27 @@
         pltpu.VMEM((2, 3, 3, 16, PART), BF),
         pltpu.VMEM((4, 4, PADBITS, 128), F32),
         pltpu.SemaphoreType.DMA((16,)),
-        pltpu.SemaphoreType.DMA((REMOTE,)),
-        pltpu.SemaphoreType.DMA((REMOTE,)),
+        pltpu.SemaphoreType.DMA((DEPARTURES,)),
+        pltpu.SemaphoreType.DMA((ARRIVALS,)),
     ]
-    grad_up, grad_down, fg, pen = pl.pallas_call(
+    grads, fg, pen = pl.pallas_call(
         fused,
         out_shape=(
-            jax.ShapeDtypeStruct((16, D), F32),
-            jax.ShapeDtypeStruct((16, D), F32),
-            jax.ShapeDtypeStruct((PADBITS, BLOCK), F32),
-            jax.ShapeDtypeStruct((8, 128), F32),
+            jax.ShapeDtypeStruct((32, D), F32),
+            jax.ShapeDtypeStruct((BITS, 1, BLOCK), F32),
+            jax.ShapeDtypeStruct((1, 1), F32),
         ),
-        in_specs=[anywhere] * 5 + [vmem] * 3 + [anywhere] * 4,
-        out_specs=(vmem,) * 4,
+        in_specs=[anywhere] * 5 + [vmem, smem, vmem] + [anywhere] * 4,
+        out_specs=(vmem,) * 3,
         scratch_shapes=scratch,
         compiler_params=pltpu.CompilerParams(
             collective_id=0, has_side_effects=True, vmem_limit_bytes=60 * 1024 * 1024
         ),
     )(
-        frames.reshape(BLOCK, D), w_query, w_key, w_value, w_out, wct, bias, wexp,
+        frames.reshape(BLOCK, D), w_query, w_key, w_value, w_out, w_code.T, code_bias, w_expand,
         w_up, w_down, decoder_stream.reshape(BLOCK, D), cotangent.reshape(BLOCK, D),
     )
-    return grad_up, grad_down, fg[:BITS].T.reshape(1, BLOCK, BITS), pen[0, 0]
+    return grads[:16], grads[16:], jnp.transpose(fg, (1, 2, 0)), pen[0, 0]
 
 
 def solution(mesh):

time: 95.8 us -> 86.8 us (0.906)
  local copies, waits for them, and re-layouts: 10.1 us -> 3.01 us
  Pallas kernels: 84.6 us -> 81.1 us
  between operations: 0.64 us -> 2.41 us
    pallas_call x1, Pallas kernels: 84.6 us -> 81.1 us  [body(): pl.pallas_call(fused, out_shape=(jax.ShapeDtypeStruct((32, D), F32), jax....]
    pad x2 -> x0, local copies, waits for them, and re-layouts: 3.07 us -> none  [the longest x1 1.53 us: body(): wct = jnp.pad(w_code.T, ((0, spare), (0, 0)))]
    unnamed x3 -> x1, local copies, waits for them, and re-layouts: 3.73 us -> 1.39 us
    reshape x3 -> x0, local copies, waits for them, and re-layouts: 2.15 us -> none  [the longest x2 1.35 us: body(): bias = jnp.pad(code_bias, (0, spare)).reshape(PADBITS, 1)]
where the time goes in v3:
time: 86.8 us; the launch traced here: 86.5 us
  Pallas kernels  81.1 us (93%)
  local copies, waits for them, and re-layouts  3.01 us (3%)
  between operations  2.41 us (3%)
    pallas_call x1, Pallas kernels, body(): pl.pallas_call(fused, out_shape=(jax.ShapeDtypeStruct((32, D), F32), jax....  81.1 us

profile of v3, /device:TPU:0, one launch (start us, length us, event | category | flops | bytes accessed | tf_op | source)
XLA Modules:
  0.0 86.5 jit_solution(14068267324933872894)
XLA Ops:
  0.6 81.1 %shard_map.147 = (f32[32,1536]{1,0:T(8,128)}, f32[18,1,512]{2,1,0:T(1,128)}, f32[1,1]{1,0:T(1,128)}) custom-call(bf16[512,1536]{1,0:T(8,128)(2,1)} %bitcast.6, bf16[1536,768]{1,0:T(8,128)(2,1)} %wq.1, bf16[1536,768]{1,0:T(8,128)(2,1)} %wk.1, bf16[1536,768]{1,0:T(8,128)(2,1)} %wv.1, bf16[768,1536]{1,0:T(8,128)(2,1)} %wo.1, bf16[18,1536]{1,0:T(8,128)(2,1)} %bitcast.9, ...), custom_call_target="tpu_custom_call" | custom-call | tf_op jit(solution)/shard_map/pallas_call | solution.py:564
  81.7 1.6 %fusion = (f32[16,1536]{1,0:T(8,128)}, f32[16,1536]{1,0:T(8,128)}) fusion(f32[32,1536]{1,0:T(8,128)} %get-tuple-element.7), kind=kLoop, calls=%fused_computation | loop fusion | bytes 393216 | tf_op jit(solution)/shard_map/slice | solution.py:581
  83.3 1.4 %copy.18 = f32[1,512,18]{1,0,2:T(1,128)} copy(f32[1,512,18]{1,0,2:T(1,128)} %bitcast.10) | data formatting | bytes 73728

commit v4 on v3

--- a/solution.py
+++ b/solution.py
@@ -457,9 +457,8 @@
     gather_end("dn")
     dpre_all()
     for p in range(3):
+        gradient(dpre, st, gu_all, p)
         forward_sum(0, p)
-    for p in range(3):
-        gradient(dpre, st, gu_all, p)
         first_sends(1, p)
     ps_send(2, "y", ps_sum(1))
     back = nt(wexp[...], up_all[...]).astype(BF)

time: 86.8 us -> 86.3 us (level)
  no operation moved by 1% of the time
where the time goes in v4:
time: 86.3 us; the launch traced here: 86 us
  Pallas kernels  80.6 us (93%)
  local copies, waits for them, and re-layouts  3.01 us (3%)
  between operations  2.41 us (3%)
    pallas_call x1, Pallas kernels, body(): pl.pallas_call(fused, out_shape=(jax.ShapeDtypeStruct((32, D), F32), jax....  80.6 us

profile of v4, /device:TPU:0, one launch (start us, length us, event | category | flops | bytes accessed | tf_op | source)
XLA Modules:
  0.0 86.0 jit_solution(1181430696516078854)
XLA Ops:
  0.6 80.6 %shard_map.147 = (f32[32,1536]{1,0:T(8,128)}, f32[18,1,512]{2,1,0:T(1,128)}, f32[1,1]{1,0:T(1,128)}) custom-call(bf16[512,1536]{1,0:T(8,128)(2,1)} %bitcast.6, bf16[1536,768]{1,0:T(8,128)(2,1)} %wq.1, bf16[1536,768]{1,0:T(8,128)(2,1)} %wk.1, bf16[1536,768]{1,0:T(8,128)(2,1)} %wv.1, bf16[768,1536]{1,0:T(8,128)(2,1)} %wo.1, bf16[18,1536]{1,0:T(8,128)(2,1)} %bitcast.9, ...), custom_call_target="tpu_custom_call" | custom-call | tf_op jit(solution)/shard_map/pallas_call | solution.py:563
  81.2 1.6 %fusion = (f32[16,1536]{1,0:T(8,128)}, f32[16,1536]{1,0:T(8,128)}) fusion(f32[32,1536]{1,0:T(8,128)} %get-tuple-element.7), kind=kLoop, calls=%fused_computation | loop fusion | bytes 393216 | tf_op jit(solution)/shard_map/slice | solution.py:580
  82.8 1.4 %copy.18 = f32[1,512,18]{1,0,2:T(1,128)} copy(f32[1,512,18]{1,0,2:T(1,128)} %bitcast.10) | data formatting | bytes 73728

commit v5 on v4

--- a/solution.py
+++ b/solution.py
@@ -25,7 +25,7 @@
 
 ORDER = (("x", "y", "z"), ("y", "z", "x"), ("z", "x", "y"))
 AXES = ("y", "z", "x")
-ARRIVALS = 58
+ARRIVALS = 70
 DEPARTURES = 17
 SHARE = INNER // 16
 
@@ -107,8 +107,9 @@
     def cols(p):
         return pl.ds(p * PART, PART)
 
-    def at(buf, p, fixed):
-        return buf.at[tuple(fixed.get(a, slice(None)) for a in AXES) + (slice(None), cols(p))]
+    def at(buf, p, fixed, lo=0, w=PART):
+        place = tuple(fixed.get(a, slice(None)) for a in AXES)
+        return buf.at[place + (slice(None), pl.ds(p * PART + lo, w))]
 
     barrier = pltpu.get_barrier_semaphore()
     others = [(lax.rem(t + j, 16), b) for j in range(1, 16)]
@@ -131,11 +132,11 @@
 
     shards = {"up": (wup, up), "dn": (wdn, dn)}
 
-    def half(buf, p, axis, n, h):
+    def half(buf, p, axis, n, h, lo=0, w=PART):
         fixed = {a: slice(None) for a in AXES}
         fixed[axis] = n
         fixed[ORDER[p][0]] = pl.ds(2 * h, 2)
-        return at(buf, p, fixed)
+        return at(buf, p, fixed, lo, w)
 
     for m in ("up", "dn"):
         src, buf = shards[m]
@@ -265,7 +266,6 @@
         return carry
 
     lax.fori_loop(0, HEADS, carry_in, 0)
-
     def out_tile(i, carry):
         rows = pl.ds(pl.multiple_of(i * 256, 256), 256)
         hid[rows, :] = (fr[rows, :].astype(F32) + nn(q[rows, :], o_w[...])).astype(BF)
@@ -276,6 +276,7 @@
     zvals = zt[...]
     code[0] = jnp.tanh(zvals).astype(BF)
     send(code.at[0], code.at[1], partner, "code", "code")
+
 
     gather_last("up")
     gather_third("dn", False)
@@ -369,54 +370,61 @@
     gd_all = gd.reshape(UNITS, D)
     gu_all = gu.reshape(UNITS, D)
 
-    def gradient(left, right, out, p):
+    def gradient(left, right, out, p, lo, w):
         def tile(i, carry):
-            cs = pl.ds(pl.multiple_of(p * PART + i * 256, 256), 256)
+            cs = pl.ds(pl.multiple_of(p * PART + lo + i * 256, 256), 256)
             out[:, cs] = nn(left[...], right[:, cs]).astype(BF)
             return carry
 
-        lax.fori_loop(0, PART // 256, tile, 0)
+        lax.fori_loop(0, w // 256, tile, 0)
 
     grads = (gd, gu)
-
-    def landing(m, p, slot, h):
-        if p == 0:
-            return r1.at[m, p, slot, :, pl.ds(2 * h, 2)]
-        return r1.at[m, p, slot, pl.ds(2 * h, 2)] if p == 1 else r1.at[m, p, slot, pl.ds(2 * h, 2)]
-
-    def first_sends(m, p):
+    first_chunks = [(0, p, 0, PART) for p in range(3)]
+    last_chunks = [(1, p, lo, 256) for lo in (0, 256) for p in range(3)]
+
+    def landing(chunk, slot, h):
+        m, p, lo, w = chunk
+        two = pl.ds(2 * h, 2)
+        place = (slice(None), two) if p == 0 else (two, slice(None))
+        return r1.at[(m, p, slot) + place + (slice(None), pl.ds(lo, w))]
+
+    def first_sends(chunk):
+        m, p, lo, w = chunk
         axis = ORDER[p][2]
         for step in (1, -1):
             h = int(step == -1)
-            block = half(grads[m], p, axis, shifted(axis, 2), h)
-            send(block, landing(m, p, 0, h), peer(axis, step), ("far", m, p), ("rs1", m))
+            block = half(grads[m], p, axis, shifted(axis, 2), h, lo, w)
+            send(block, landing(chunk, 0, h), peer(axis, step), ("far", chunk), ("rs1", m))
         for step in (1, -1):
             h = int(step == 1)
             slot = 1 if step == 1 else 2
-            block = half(grads[m], p, axis, shifted(axis, step), h)
-            send(block, landing(m, p, slot, h), peer(axis, step), ("near", m, p), ("rs1", m))
-
-    def forward_sum(m, p):
+            block = half(grads[m], p, axis, shifted(axis, step), h, lo, w)
+            send(block, landing(chunk, slot, h), peer(axis, step), ("near", chunk), ("rs1", m))
+
+    def forward_sum(chunk):
+        m, p, lo, w = chunk
         axis = ORDER[p][2]
-        arrived(("far", m, p), r1.at[m, p, 0])
+        arrived(("far", chunk), r1.at[m, p, 0, :, :, :, pl.ds(lo, w)])
         for step in (1, -1):
             h = int(step == -1)
             slot = 1 if step == 1 else 2
-            block = half(grads[m], p, axis, shifted(axis, step), h)
-            came = landing(m, p, 0, h)
+            block = half(grads[m], p, axis, shifted(axis, step), h, lo, w)
+            came = landing(chunk, 0, h)
             block[...] = (block[...].astype(F32) + came[...].astype(F32)).astype(BF)
-            send(block, landing(m, p, slot, h), peer(axis, step), ("near", m, p), ("rs1", m))
-
-    def second_sends(m, p):
+            send(block, landing(chunk, slot, h), peer(axis, step), ("near", chunk), ("rs1", m))
+
+    def second_sends(chunk):
+        m, p, lo, w = chunk
         axis = ORDER[p][2]
-        arrived(("near", m, p), r1.at[m, p, pl.ds(1, 2)])
-        block = at(grads[m], p, {axis: pos[axis]})
+        cs = pl.ds(lo, w)
+        arrived(("near", chunk), r1.at[m, p, pl.ds(1, 2), :, :, :, cs])
+        block = at(grads[m], p, {axis: pos[axis]}, lo, w)
 
         def total1(i, carry):
-            s1[m, p, i] = (
+            s1[m, p, i, :, :, cs] = (
                 block[i].astype(F32)
-                + r1[m, p, 1, i].astype(F32)
-                + r1[m, p, 2, i].astype(F32)
+                + r1[m, p, 1, i, :, :, cs].astype(F32)
+                + r1[m, p, 2, i, :, :, cs].astype(F32)
             ).astype(BF)
             return carry
 
@@ -424,58 +432,68 @@
         axis = ORDER[p][1]
         for step in (2, 1, 3):
             n = shifted(axis, step)
-            src = s1.at[m, p, n] if p == 0 else s1.at[m, p, :, n]
-            send(src, r2.at[m, p, step - 1], peer(axis, step), ("rs2", m, p), "rs2")
-
-    def third_sends(m, p):
+            src = s1.at[m, p, n, :, :, cs] if p == 0 else s1.at[m, p, :, n, :, cs]
+            send(src, r2.at[m, p, step - 1, :, :, cs], peer(axis, step), ("rs2", chunk), "rs2")
+
+    def third_sends(chunk):
+        m, p, lo, w = chunk
         axis = ORDER[p][1]
-        arrived(("rs2", m, p), r2.at[m, p])
-        mine = s1.at[m, p, pos[axis]] if p == 0 else s1.at[m, p, :, pos[axis]]
+        cs = pl.ds(lo, w)
+        arrived(("rs2", chunk), r2.at[m, p, :, :, :, cs])
+        n = pos[axis]
+        mine = s1.at[m, p, n, :, :, cs] if p == 0 else s1.at[m, p, :, n, :, cs]
         total = mine[...].astype(F32)
         for step in range(3):
-            total = total + r2[m, p, step].astype(F32)
-        s2[m, p] = total.astype(BF)
+            total = total + r2[m, p, step, :, :, cs].astype(F32)
+        s2[m, p, :, :, cs] = total.astype(BF)
         axis = ORDER[p][0]
         for step in (2, 1, 3):
-            src = s2.at[m, p, shifted(axis, step)]
-            send(src, r3.at[m, p, step - 1], peer(axis, step), ("rs3", m, p), "rs3")
+            src = s2.at[m, p, shifted(axis, step), :, cs]
+            send(src, r3.at[m, p, step - 1, :, cs], peer(axis, step), ("rs3", chunk), "rs3")
 
     scale = 1.0 / math.sqrt(TOTAL)
 
-    def last_sum(m, p):
+    def last_sum(chunk):
+        m, p, lo, w = chunk
         axis = ORDER[p][0]
-        total = s2[m, p, pos[axis]].astype(F32)
-        arrived(("rs3", m, p), r3.at[m, p])
+        cs = pl.ds(lo, w)
+        total = s2[m, p, pos[axis], :, cs].astype(F32)
+        arrived(("rs3", chunk), r3.at[m, p, :, :, cs])
         for step in range(3):
-            total = total + r3[m, p, step].astype(F32)
-        grad_out[pl.ds(16 * (1 - m), 16), cols(p)] = total * scale
+            total = total + r3[m, p, step, :, cs].astype(F32)
+        grad_out[pl.ds(16 * (1 - m), 16), pl.ds(p * PART + lo, w)] = total * scale
 
     arrived("cot", ct.at[there])
-    for p in range(3):
-        gradient(act, ct, gd_all, p)
-        first_sends(0, p)
+    for chunk in first_chunks:
+        gradient(act, ct, gd_all, *chunk[1:])
+        first_sends(chunk)
     gather_end("dn")
     dpre_all()
-    for p in range(3):
-        gradient(dpre, st, gu_all, p)
-        forward_sum(0, p)
-        first_sends(1, p)
+    for i, chunk in enumerate(last_chunks):
+        gradient(dpre, st, gu_all, *chunk[1:])
+        if i in (1, 3, 5):
+            forward_sum(first_chunks[i // 2])
+        first_sends(chunk)
+
     ps_send(2, "y", ps_sum(1))
     back = nt(wexp[...], up_all[...]).astype(BF)
-
     for i in range(4):
         dc[:, tiles[i]] = nn(back, dpre[:, tiles[i]])
     send(dc.at[:, there], dc_recv, partner, "dc", "dc")
     ps_send(3, "z", ps_sum(2))
 
-    for p in range(3):
-        second_sends(0, p)
-    for p in range(3):
-        forward_sum(1, p)
-    for p in range(3):
-        third_sends(0, p)
-    for p in range(3):
-        second_sends(1, p)
+    for chunk in last_chunks[:3]:
+        forward_sum(chunk)
+    for chunk in first_chunks:
+        second_sends(chunk)
+    for chunk in last_chunks[3:]:
+        forward_sum(chunk)
+    for chunk in last_chunks[:3]:
+        second_sends(chunk)
+    for chunk in first_chunks:
+        third_sends(chunk)
+    for chunk in last_chunks[3:]:
+        second_sends(chunk)
 
     arrived("dc", dc_recv)
     sums_all = ps_sum(3)
@@ -495,12 +513,14 @@
     for i in range(BITS):
         fg_out[i] = fg[i : i + 1, :]
 
-    for p in range(3):
-        last_sum(0, p)
-    for p in range(3):
-        third_sends(1, p)
-    for p in range(3):
-        last_sum(1, p)
+    for chunk in last_chunks[:3]:
+        third_sends(chunk)
+    for chunk in first_chunks:
+        last_sum(chunk)
+    for chunk in last_chunks[3:]:
+        third_sends(chunk)
+    for chunk in last_chunks:
+        last_sum(chunk)
     for departure, size in (
         ("ag1", r3), ("ag2", r2), (("ag3", "up"), r1.at[0]), (("ag3", "dn"), r1.at[0]),
         ("tokens", ct), ("a1", prefix.at[pl.ds(0, 15)]), ("a2", prefix.at[pl.ds(0, 15)]),

time: 86.3 us -> 85.9 us (level)
  no operation moved by 1% of the time
where the time goes in v5:
time: 85.9 us; the launch traced here: 85.6 us
  Pallas kernels  80.2 us (93%)
  local copies, waits for them, and re-layouts  3.01 us (4%)
  between operations  2.41 us (3%)
    pallas_call x1, Pallas kernels, body(): pl.pallas_call(fused, out_shape=(jax.ShapeDtypeStruct((32, D), F32), jax....  80.2 us

profile of v5, /device:TPU:0, one launch (start us, length us, event | category | flops | bytes accessed | tf_op | source)
XLA Modules:
  0.0 85.6 jit_solution(1500241639254409516)
XLA Ops:
  0.6 80.2 %shard_map.147 = (f32[32,1536]{1,0:T(8,128)}, f32[18,1,512]{2,1,0:T(1,128)}, f32[1,1]{1,0:T(1,128)}) custom-call(bf16[512,1536]{1,0:T(8,128)(2,1)} %bitcast.6, bf16[1536,768]{1,0:T(8,128)(2,1)} %wq.1, bf16[1536,768]{1,0:T(8,128)(2,1)} %wk.1, bf16[1536,768]{1,0:T(8,128)(2,1)} %wv.1, bf16[768,1536]{1,0:T(8,128)(2,1)} %wo.1, bf16[18,1536]{1,0:T(8,128)(2,1)} %bitcast.9, ...), custom_call_target="tpu_custom_call" | custom-call | tf_op jit(solution)/shard_map/pallas_call | solution.py:583
  80.9 1.6 %fusion = (f32[16,1536]{1,0:T(8,128)}, f32[16,1536]{1,0:T(8,128)}) fusion(f32[32,1536]{1,0:T(8,128)} %get-tuple-element.7), kind=kLoop, calls=%fused_computation | loop fusion | bytes 393216 | tf_op jit(solution)/shard_map/slice | solution.py:600
  82.5 1.4 %copy.18 = f32[1,512,18]{1,0,2:T(1,128)} copy(f32[1,512,18]{1,0,2:T(1,128)} %bitcast.10) | data formatting | bytes 73728
